TPU v7x, 256 devices: a whole 4x4x8 slice. The times are simulated.
256 devices in a mesh: level: 4 (over x), wide: 64 (over y, z, core).
Axes of the slice: x: 4, y: 4, z: 8, core: 2. Of those that a mesh axis runs over, the one named last changes fastest.
Arguments:
- coarse_input: bfloat16 [256, 51200], P('wide', 'level'), may hold values from -6 to 6
- fine_input: bfloat16 [4, 128, 32768], P('level', 'wide'), may hold values from -6 to 6
- coarse_cotangent: float32 [256, 12800], P('wide', 'level'), may hold values from -6 to 6
- fine_cotangent: float32 [4, 128, 8192], P('level', 'wide'), may hold values from -6 to 6
- well_x: int32 [4], replicated, may hold values from 0 to 192
- well_y: int32 [4], replicated, may hold values from 0 to 24
- coarse_lift: bfloat16 [4, 48], replicated, may hold values from -3 to 3
- coarse_mixing: bfloat16 [48, 48], replicated, may hold values from -0.875 to 0.875
- coarse_spectral: bfloat16 [512, 32, 2, 2304], P(('level', 'wide')), may hold values from -8 to 8
- coarse_readout: bfloat16 [48], replicated, may hold values from -2 to 2
- fine_lift: bfloat16 [4, 5, 48], P('level'), may hold values from -2.5 to 2.5
- fine_mixing: bfloat16 [4, 48, 48], P('level'), may hold values from -0.875 to 0.875
- fine_spectral: bfloat16 [4, 512, 32, 2, 2304], P('level', 'wide'), may hold values from -6 to 6
- fine_readout: bfloat16 [4, 48], P('level'), may hold values from -2 to 2
Outputs:
- coarse_pred: bfloat16 [256, 12800], P('wide', 'level')
- fine_pred: bfloat16 [4, 128, 8192], P('level', 'wide')
- coarse_grad: float32 [512, 32, 2, 2304], P(('level', 'wide'))
- fine_grad: float32 [4, 512, 32, 2, 2304], P('level', 'wide')
Inputs may be any that keep to these rules, and one draw needn't show every extreme that they name: Level l's box covers 128 // 2 global planes from well_x[l] on. Level l's box covers 128 // 2 global rows from 8 well_y[l] on.
All inputs are finite; a program needn't handle non-finite values.
Results may differ from a plain program's by a relative error of at most 0.014.
Values may be sent and summed in bfloat16 or wider, within the bound.
A program may use at most 128 MiB of HBM per device.

v0:
```python
import math

import jax
import jax.numpy as jnp
from jax import lax
from jax.sharding import PartitionSpec as P

MODES = 16
CIN = 4
GX = 256
GY = 256
GZ = 50
FX = 128
FY = 128
FZ = 64
YB = 8


HIGH = lax.Precision.HIGHEST


def waves(row_ids, freq_ids, length):
    signed = jnp.where(freq_ids < MODES, freq_ids, freq_ids - 2 * MODES)
    product = jnp.mod(row_ids[:, None] * signed[None, :], length)
    angles = product.astype(jnp.float32) * (2.0 * math.pi / length)
    factor = 1.0 / math.sqrt(length)
    return (jnp.cos(angles) * factor, jnp.sin(angles) * factor)


def depth_table(length):
    cosine, sine_part = waves(
        jnp.arange(length, dtype=jnp.int32), jnp.arange(MODES, dtype=jnp.int32), length
    )
    return jnp.concatenate([cosine, -sine_part], axis=1)


def along_y(spectra, cosine, sine_part):
    parts = spectra.reshape(spectra.shape[0], spectra.shape[1], 2, MODES, spectra.shape[3])
    table = jnp.stack(
        [jnp.stack([cosine, -sine_part], axis=1), jnp.stack([sine_part, cosine], axis=1)], axis=1
    )
    return jnp.einsum("xypkc,ypqj->jkxqc", parts, table, precision=HIGH)


def back_y(pieces, cosine, sine_part):
    table = jnp.stack(
        [jnp.stack([cosine, sine_part], axis=1), jnp.stack([-sine_part, cosine], axis=1)], axis=1
    )
    result = jnp.einsum("jkxqc,yqpj->xypkc", pieces, table, precision=HIGH)
    return result.reshape(result.shape[0], result.shape[1], 2 * MODES, result.shape[4])


def along_x(blocks):
    length = blocks.shape[1]
    cosine, sine_part = waves(
        jnp.arange(length, dtype=jnp.int32), jnp.arange(2 * MODES, dtype=jnp.int32), length
    )
    real_part = blocks[:, :, 0]
    imag_part = blocks[:, :, 1]
    out_real = jnp.einsum("mxc,xj->mjc", real_part, cosine, precision=HIGH) + jnp.einsum(
        "mxc,xj->mjc", imag_part, sine_part, precision=HIGH
    )
    out_imag = jnp.einsum("mxc,xj->mjc", imag_part, cosine, precision=HIGH) - jnp.einsum(
        "mxc,xj->mjc", real_part, sine_part, precision=HIGH
    )
    return jnp.stack([out_real, out_imag], axis=2)


def back_x(spectra, length):
    cosine, sine_part = waves(
        jnp.arange(length, dtype=jnp.int32), jnp.arange(2 * MODES, dtype=jnp.int32), length
    )
    real_part = spectra[:, :, 0]
    imag_part = spectra[:, :, 1]
    out_real = jnp.einsum("mjc,xj->mxc", real_part, cosine, precision=HIGH) - jnp.einsum(
        "mjc,xj->mxc", imag_part, sine_part, precision=HIGH
    )
    out_imag = jnp.einsum("mjc,xj->mxc", imag_part, cosine, precision=HIGH) + jnp.einsum(
        "mjc,xj->mxc", real_part, sine_part, precision=HIGH
    )
    return jnp.stack([out_real, out_imag], axis=2)


def mixed(spectra, weights):
    real_part = spectra[:, :, 0]
    imag_part = spectra[:, :, 1]
    weight_real = weights[:, :, 0]
    weight_imag = weights[:, :, 1]
    out_real = jnp.einsum("mjc,mjcd->mjd", real_part, weight_real, precision=HIGH) - jnp.einsum(
        "mjc,mjcd->mjd", imag_part, weight_imag, precision=HIGH
    )
    out_imag = jnp.einsum("mjc,mjcd->mjd", real_part, weight_imag, precision=HIGH) + jnp.einsum(
        "mjc,mjcd->mjd", imag_part, weight_real, precision=HIGH
    )
    return jnp.stack([out_real, out_imag], axis=2)


def mixed_adjoint(spectra, weights):
    real_part = spectra[:, :, 0]
    imag_part = spectra[:, :, 1]
    weight_real = weights[:, :, 0]
    weight_imag = weights[:, :, 1]
    out_real = jnp.einsum("mjd,mjcd->mjc", real_part, weight_real, precision=HIGH) + jnp.einsum(
        "mjd,mjcd->mjc", imag_part, weight_imag, precision=HIGH
    )
    out_imag = jnp.einsum("mjd,mjcd->mjc", imag_part, weight_real, precision=HIGH) - jnp.einsum(
        "mjd,mjcd->mjc", real_part, weight_imag, precision=HIGH
    )
    return jnp.stack([out_real, out_imag], axis=2)


def weight_grads(source, target):
    source_real = source[:, :, 0]
    source_imag = source[:, :, 1]
    target_real = target[:, :, 0]
    target_imag = target[:, :, 1]
    grad_real = jnp.einsum("mjc,mjd->mjcd", source_real, target_real, precision=HIGH) + jnp.einsum(
        "mjc,mjd->mjcd", source_imag, target_imag, precision=HIGH
    )
    grad_imag = jnp.einsum("mjc,mjd->mjcd", source_real, target_imag, precision=HIGH) - jnp.einsum(
        "mjc,mjd->mjcd", source_imag, target_real, precision=HIGH
    )
    stacked = jnp.stack([grad_real, grad_imag], axis=2)
    return stacked.reshape(
        stacked.shape[0], stacked.shape[1], 2, stacked.shape[3] * stacked.shape[4]
    )


def to_modes(blocks):
    return along_x(lax.all_to_all(blocks, "wide", split_axis=0, concat_axis=1, tiled=True))


def from_modes(spectra, length):
    return lax.all_to_all(back_x(spectra, length), "wide", split_axis=1, concat_axis=0, tiled=True)


def shards(
    coarse_input,
    fine_input,
    coarse_cotangent,
    fine_cotangent,
    well_x,
    well_y,
    coarse_lift,
    coarse_mixing,
    coarse_spectral,
    coarse_readout,
    fine_lift,
    fine_mixing,
    fine_spectral,
    fine_readout,
):
    level_count = lax.axis_size("level")
    wide_count = lax.axis_size("wide")
    level_index = lax.axis_index("level")
    wide_index = lax.axis_index("wide")
    planes = coarse_input.shape[0]
    rows_here = coarse_input.shape[1] // (GZ * CIN)
    channels = coarse_mixing.shape[0]
    fine_planes = fine_input.shape[1]
    per_level = 2 * MODES // level_count
    block_rows = rows_here // YB
    box_blocks = FY // 2 // YB
    per_owner = fine_planes // 2
    block_size = YB * GZ
    coarse_table = depth_table(GZ)
    coarse_bf = coarse_table.astype(jnp.bfloat16)
    row_ids = level_index * rows_here + jnp.arange(rows_here, dtype=jnp.int32)
    zero_bf = jnp.zeros((), jnp.bfloat16)

    def coarse_forward(grid_field):
        spectra = jnp.einsum(
            "xyzc,zk->xykc", grid_field, coarse_bf, preferred_element_type=jnp.float32
        )
        freq_ids = jnp.arange(lax.axis_size("level") * per_level, dtype=jnp.int32)
        cosine, sine_part = waves(row_ids, freq_ids, GY)
        kept_rows = lax.psum_scatter(
            along_y(spectra, cosine, sine_part), "level", scatter_dimension=0, tiled=True
        )
        return to_modes(kept_rows.reshape(per_level * MODES, planes, 2, channels))

    coarse_weights = coarse_spectral.astype(jnp.float32).reshape(
        coarse_spectral.shape[0], 2 * MODES, 2, channels, channels
    )
    coarse_features = coarse_input.reshape(planes, rows_here, GZ, CIN)
    lifted = jnp.einsum(
        "xyzi,ic->xyzc", coarse_features, coarse_lift, preferred_element_type=jnp.float32
    ).astype(jnp.bfloat16)
    coarse_modes = coarse_forward(lifted)
    returned = from_modes(mixed(coarse_modes, coarse_weights), GX).reshape(
        per_level, MODES, planes, 2, channels
    )
    portion = lax.all_gather(returned, "level", axis=0, tiled=True)
    cosine, sine_part = waves(row_ids, jnp.arange(portion.shape[0], dtype=jnp.int32), GY)
    spectral_y = back_y(portion, cosine, sine_part).astype(jnp.bfloat16)
    coarse_pre = jnp.einsum(
        "xykc,zk->xyzc", spectral_y, coarse_bf, preferred_element_type=jnp.float32
    ) + jnp.einsum("xyzc,cd->xyzd", lifted, coarse_mixing, preferred_element_type=jnp.float32)
    coarse_hidden, coarse_slope = jax.vjp(jax.nn.gelu, coarse_pre)
    coarse_out = jnp.einsum(
        "xyzc,c->xyz",
        coarse_hidden.astype(jnp.bfloat16),
        coarse_readout,
        preferred_element_type=jnp.float32,
    ).astype(jnp.bfloat16)
    coarse_blocks = coarse_out.reshape(planes * block_rows, block_size)
    dest_wide = jnp.arange(wide_count, dtype=jnp.int32)[None, :, None]
    slot_ids = jnp.arange(per_owner * box_blocks, dtype=jnp.int32)[None, None, :]
    plane_ids = (
        well_x[:, None, None] + dest_wide * per_owner + slot_ids // box_blocks - wide_index * planes
    )
    row_blocks = well_y[:, None, None] + slot_ids % box_blocks - level_index * block_rows
    is_owned = (
        (plane_ids >= 0) & (plane_ids < planes) & (row_blocks >= 0) & (row_blocks < block_rows)
    )
    pick_rows = jnp.clip(plane_ids, 0, planes - 1) * block_rows + jnp.clip(
        row_blocks, 0, block_rows - 1
    )
    outgoing = jnp.where(is_owned[..., None], coarse_blocks[pick_rows], zero_bf)
    arrived = lax.all_to_all(
        lax.all_to_all(outgoing, "level", split_axis=0, concat_axis=0, tiled=True),
        "wide",
        split_axis=1,
        concat_axis=1,
        tiled=True,
    )
    coarse_slab = jnp.sum(arrived, axis=(0, 1))
    depth_map = (jnp.arange(FZ, dtype=jnp.int32) * GZ // FZ)[None, :] == jnp.arange(
        GZ, dtype=jnp.int32
    )[:, None]
    slab_grid = coarse_slab.reshape(per_owner, box_blocks * YB, GZ)
    refined = jnp.einsum(
        "xyg,gf->xyf", slab_grid, depth_map.astype(jnp.bfloat16), preferred_element_type=jnp.float32
    ).astype(jnp.bfloat16)
    refined = jnp.repeat(jnp.repeat(refined, 2, axis=0), 2, axis=1)
    fine_table = depth_table(FZ)
    fine_bf = fine_table.astype(jnp.bfloat16)
    fine_cos, fine_sin = waves(
        jnp.arange(FY, dtype=jnp.int32), jnp.arange(2 * MODES, dtype=jnp.int32), FY
    )

    def fine_forward(grid_field):
        spectra = jnp.einsum(
            "xyzc,zk->xykc", grid_field, fine_bf, preferred_element_type=jnp.float32
        )
        return to_modes(
            along_y(spectra, fine_cos, fine_sin).reshape(
                2 * MODES * MODES, fine_planes, 2, channels
            )
        )

    def fine_inverse(spectra):
        columns = from_modes(spectra, FX).reshape(2 * MODES, MODES, fine_planes, 2, channels)
        spectral = back_y(columns, fine_cos, fine_sin).astype(jnp.bfloat16)
        return jnp.einsum("xykc,zk->xyzc", spectral, fine_bf, preferred_element_type=jnp.float32)

    fine_features = fine_input[0].reshape(fine_planes, FY, FZ, CIN)
    stacked = jnp.concatenate([fine_features, refined[..., None]], axis=3)
    fine_lifted = jnp.einsum(
        "xyzi,ic->xyzc", stacked, fine_lift[0], preferred_element_type=jnp.float32
    ).astype(jnp.bfloat16)
    fine_weights = (
        fine_spectral[0]
        .astype(jnp.float32)
        .reshape(fine_spectral.shape[1], 2 * MODES, 2, channels, channels)
    )
    fine_modes = fine_forward(fine_lifted)
    fine_pre = fine_inverse(mixed(fine_modes, fine_weights)) + jnp.einsum(
        "xyzc,cd->xyzd", fine_lifted, fine_mixing[0], preferred_element_type=jnp.float32
    )
    fine_hidden, fine_slope = jax.vjp(jax.nn.gelu, fine_pre)
    fine_out = jnp.einsum(
        "xyzc,c->xyz",
        fine_hidden.astype(jnp.bfloat16),
        fine_readout[0],
        preferred_element_type=jnp.float32,
    ).astype(jnp.bfloat16)
    fine_pull = fine_cotangent[0].reshape(fine_planes, FY, FZ)[..., None] * fine_readout[0].astype(
        jnp.float32
    )
    fine_push = fine_slope(fine_pull)[0].astype(jnp.bfloat16)
    fine_dual = fine_forward(fine_push)
    fine_grad = weight_grads(fine_modes, fine_dual)
    fine_back = fine_inverse(mixed_adjoint(fine_dual, fine_weights)) + jnp.einsum(
        "xyzd,cd->xyzc", fine_push, fine_mixing[0], preferred_element_type=jnp.float32
    )
    coarse_part = jnp.sum(fine_back * fine_lift[0, CIN].astype(jnp.float32), axis=-1)
    pooled = coarse_part.reshape(per_owner, 2, FY // 2, 2, FZ).sum(axis=(1, 3))
    pooled = jnp.einsum(
        "xyf,gf->xyg", pooled, depth_map.astype(jnp.float32), precision=HIGH
    ).reshape(per_owner * box_blocks, block_size)
    corner_x = well_x[level_index]
    corner_y = well_y[level_index]
    slot_ids = jnp.arange(per_owner * box_blocks, dtype=jnp.int32)
    plane_global = corner_x + wide_index * per_owner + slot_ids // box_blocks
    block_global = corner_y + slot_ids % box_blocks
    owner_wide = plane_global // planes
    owner_level = block_global // block_rows
    targets = (
        jnp.arange(level_count, dtype=jnp.int32)[:, None, None] == owner_level[None, None, :]
    ) & (jnp.arange(wide_count, dtype=jnp.int32)[None, :, None] == owner_wide[None, None, :])
    outgoing = jnp.where(targets[..., None], pooled[None, None], 0.0)
    arrived = lax.all_to_all(
        lax.all_to_all(
            outgoing.astype(jnp.bfloat16), "level", split_axis=0, concat_axis=0, tiled=True
        ),
        "wide",
        split_axis=1,
        concat_axis=1,
        tiled=True,
    ).astype(outgoing.dtype)
    plane_local = (
        well_x[:, None, None]
        + jnp.arange(wide_count, dtype=jnp.int32)[None, :, None] * per_owner
        + slot_ids[None, None, :] // box_blocks
        - wide_index * planes
    )
    block_local = (
        well_y[:, None, None] + slot_ids[None, None, :] % box_blocks - level_index * block_rows
    )
    valid = (
        (plane_local >= 0)
        & (plane_local < planes)
        & (block_local >= 0)
        & (block_local < block_rows)
    )
    target_ids = plane_local * block_rows + block_local
    chooser = (
        (target_ids[..., None] == jnp.arange(planes * block_rows, dtype=jnp.int32))
        & valid[..., None]
    ).astype(jnp.float32)
    gathered_back = jnp.einsum("lwsb,lwsv->bv", chooser, arrived, precision=HIGH)
    coarse_total = coarse_cotangent.reshape(planes, rows_here, GZ) + gathered_back.reshape(
        planes, rows_here, GZ
    )
    coarse_pull = coarse_total[..., None] * coarse_readout.astype(jnp.float32)
    coarse_push = coarse_slope(coarse_pull)[0].astype(jnp.bfloat16)
    coarse_dual = coarse_forward(coarse_push)
    coarse_grad = weight_grads(coarse_modes, coarse_dual)
    return (
        coarse_out.reshape(planes, rows_here * GZ),
        fine_out.reshape(1, fine_planes, FY * FZ),
        coarse_grad,
        fine_grad[None],
    )


def solution(mesh):
    placed = (
        P("wide", "level"),
        P("level", "wide", None),
        P("wide", "level"),
        P("level", "wide", None),
        P(),
        P(),
        P(),
        P(),
        P(("level", "wide"), None, None, None),
        P(),
        P("level", None, None),
        P("level", None, None),
        P("level", "wide", None, None, None),
        P("level", None),
    )
    return jax.shard_map(
        shards,
        mesh=mesh,
        in_specs=placed,
        out_specs=(
            P("wide", "level"),
            P("level", "wide", None),
            P(("level", "wide"), None, None, None),
            P("level", "wide", None, None, None),
        ),
        check_vma=False,
    )
```

profile of v0, /device:TPU:1, one launch (start us, length us, event | category | flops | bytes accessed | tf_op | source)
XLA Modules:
  0.0 610.4 jit_solution(9757659158186977004)
XLA Ops:
  20.2 8.6 %fusion.53 = f32[32,16,4,2,48]{4,0,1,2,3:T(8,128)} fusion(f32[4,64,2,16,48]{1,3,2,4,0:T(8,128)S(1)} %bitcast.499, f32[64,1,2,32]{0,3,1,2:T(8,128)S(1)} %get-tuple-element.39, f32[64,1,2,32]{0,3,1,2:T(8,128)S(1)} %get-tuple-element.44), kind=kOutput, calls=%fused_computation.71 | convolution fusion | flops 301998080 | bytes 2392064 | tf_op jit(solution)/shard_map/xypkc,ypqj->jkxqc/dot_general | solution.py:42
  32.5 32.6 %reduce-scatter.3.cloned.1.call-done = f32[8,16,4,2,48]{4,0,1,2,3:T(8,128)} async-done(((f32[32,16,4,2,48]{4,0,1,2,3:T(8,128)}), f32[8,16,4,2,48]{4,0,1,2,3:T(8,128)}) %reduce-scatter.3.cloned.1.call-update) | async-done | bytes 196624 | tf_op jit(solution)/shard_map/reduce_scatter | solution.py:177
  68.2 10.6 %all-to-all-start = ((f32[64,1,768]{2,1,0:T(1,128)}), f32[64,1,768]{2,1,0:T(1,128)S(1)}, u32[]{:S(2)}, u32[]{:S(2)}) async-start(f32[64,1,768]{2,1,0:T(1,128)} %reshape.824), calls=%async_computation.1 | async-start | bytes 393216 | tf_op jit(solution)/shard_map/all_to_all | solution.py:130
  79.6 10.1 %all-to-all-done = f32[64,1,768]{2,1,0:T(1,128)S(1)} async-done(((f32[64,1,768]{2,1,0:T(1,128)}), f32[64,1,768]{2,1,0:T(1,128)S(1)}, u32[]{:S(2)}, u32[]{:S(2)}) %all-to-all-start) | async-done | bytes 196640 | tf_op jit(solution)/shard_map/all_to_all | solution.py:130
  111.3 7.7 %all-to-all-done.1 = f32[64,1,768]{2,1,0:T(1,128)S(1)} async-done(((f32[64,1,768]{2,1,0:T(1,128)}), f32[64,1,768]{2,1,0:T(1,128)S(1)}, u32[]{:S(2)}, u32[]{:S(2)}) %all-to-all-start.1) | async-done | bytes 196640 | tf_op jit(solution)/shard_map/all_to_all | solution.py:134
  121.6 21.0 %all_gather.3 = f32[32,16,4,2,48]{4,0,3,2,1:T(8,128)S(1)} all-gather(f32[8,16,4,2,48]{4,0,3,2,1:T(8,128)S(1)} %copy.314), channel_id=1, replica_groups=mesh['level'=4,'wide'=64] {'level'}, dimensions={0}, use_global_device_ids=true | all-gather | bytes 983040 | tf_op jit(solution)/shard_map/all_gather | solution.py:193
  152.9 7.5 %gather_fusion = bf16[2048,400]{1,0:T(8,128)(2,1)S(1)} fusion(bf16[32,400]{1,0:T(8,128)(2,1)S(1)} %reshape.747, s32[2048]{0:T(1024)S(1)} %broadcast_clamp_fusion), kind=kCustom, calls=%fused_computation | custom fusion | bytes 3284992 | tf_op jit(solution)/shard_map/gather | solution.py:219
  160.9 27.8 %all_to_all.137 = bf16[4,64,8,400]{3,2,1,0:T(8,128)(2,1)S(1)} all-to-all(bf16[4,64,8,400]{3,2,1,0:T(8,128)(2,1)S(1)} %broadcast_select_fusion), channel_id=1, replica_groups=mesh['level'=4,'wide'=64] {'level'}, dimensions={0} | all-to-all | bytes 3276800 | tf_op jit(solution)/shard_map/all_to_all | solution.py:221
  190.4 7.4 %all-to-all-start.3 = ((bf16[4,64,8,400]{3,2,0,1:T(8,128)(2,1)}), bf16[4,64,8,400]{3,2,0,1:T(8,128)(2,1)S(1)}, u32[]{:S(2)}, u32[]{:S(2)}) async-start(bf16[4,64,8,400]{3,2,0,1:T(8,128)(2,1)} %copy.321), calls=%async_computation.4 | async-start | bytes 4194304 | tf_op jit(solution)/shard_map/all_to_all | solution.py:220
  197.8 11.0 %reshape_squeeze.3 = bf16[2,128,64,4]{3,2,1,0:T(8,128)(2,1)} reshape(bf16[1,2,32768]{2,1,0:T(2,128)(2,1)S(1)} %copy-done.29) | data formatting | bytes 262144 | tf_op jit(solution)/shard_map/reshape;squeeze | solution.py:257
  215.5 33.4 %all-to-all-done.3 = bf16[4,64,8,400]{3,2,0,1:T(8,128)(2,1)S(1)} async-done(((bf16[4,64,8,400]{3,2,0,1:T(8,128)(2,1)}), bf16[4,64,8,400]{3,2,0,1:T(8,128)(2,1)S(1)}, u32[]{:S(2)}, u32[]{:S(2)}) %all-to-all-start.3) | async-done | bytes 1638432 | tf_op jit(solution)/shard_map/all_to_all | solution.py:220
  264.4 11.3 %reshape.751 = bf16[8,32,2,48,48]{4,3,2,1,0:T(8,128)(2,1)} reshape(bf16[1,8,32,2,2304]{4,3,2,1,0:T(2,128)(2,1)} %param.26) | data formatting | bytes 4718592 | tf_op jit(solution)/shard_map/reshape | solution.py:265
  307.9 7.1 %all-to-all-start.5 = ((f32[64,1,1536]{2,1,0:T(1,128)}), f32[64,1,1536]{2,1,0:T(1,128)S(1)}, u32[]{:S(2)}, u32[]{:S(2)}) async-start(f32[64,1,1536]{2,1,0:T(1,128)} %reshape.830), calls=%async_computation.6 | async-start | bytes 786432 | tf_op jit(solution)/shard_map/all_to_all | solution.py:134
  317.5 12.1 %all-to-all-done.5 = f32[64,1,1536]{2,1,0:T(1,128)S(1)} async-done(((f32[64,1,1536]{2,1,0:T(1,128)}), f32[64,1,1536]{2,1,0:T(1,128)S(1)}, u32[]{:S(2)}, u32[]{:S(2)}) %all-to-all-start.5) | async-done | bytes 393248 | tf_op jit(solution)/shard_map/all_to_all | solution.py:134
  357.2 10.4 %all-to-all-done.6 = f32[64,1,1536]{2,1,0:T(1,128)S(1)} async-done(((f32[64,1,1536]{2,1,0:T(1,128)}), f32[64,1,1536]{2,1,0:T(1,128)S(1)}, u32[]{:S(2)}, u32[]{:S(2)}) %all-to-all-start.6) | async-done | bytes 393248 | tf_op jit(solution)/shard_map/all_to_all | solution.py:130
  380.6 6.7 %fusion.41 = f32[8,32,1,48]{3,2,1,0:T(1,128)S(1)} fusion(f32[8,32,48,1]{2,3,1,0:T(1,128)S(1)} %bitcast.546, bf16[8,32,2,48,48]{4,3,2,1,0:T(8,128)(2,1)} %reshape.751), kind=kOutput, calls=%fused_computation.62 | convolution fusion | flops 7077888 | bytes 3244032 | tf_op jit(solution)/shard_map/mjd,mjcd->mjc/dot_general | solution.py:103
  402.7 6.7 %all-to-all-start.7 = ((f32[64,1,1536]{2,1,0:T(1,128)}), f32[64,1,1536]{2,1,0:T(1,128)S(1)}, u32[]{:S(2)}, u32[]{:S(2)}) async-start(f32[64,1,1536]{2,1,0:T(1,128)} %reshape.834), calls=%async_computation.8 | async-start | bytes 786432 | tf_op jit(solution)/shard_map/all_to_all | solution.py:134
  412.9 11.1 %all-to-all-done.7 = f32[64,1,1536]{2,1,0:T(1,128)S(1)} async-done(((f32[64,1,1536]{2,1,0:T(1,128)}), f32[64,1,1536]{2,1,0:T(1,128)S(1)}, u32[]{:S(2)}, u32[]{:S(2)}) %all-to-all-start.7) | async-done | bytes 393248 | tf_op jit(solution)/shard_map/all_to_all | solution.py:134
  435.3 28.5 %all_to_all.138 = bf16[4,64,8,400]{3,2,1,0:T(8,128)(2,1)S(1)} all-to-all(bf16[4,64,8,400]{3,2,1,0:T(8,128)(2,1)S(1)} %select_convert_fusion), channel_id=1, replica_groups=mesh['level'=4,'wide'=64] {'level'}, dimensions={0} | all-to-all | bytes 3276800 | tf_op jit(solution)/shard_map/all_to_all | solution.py:304
  465.5 6.9 %all-to-all-start.9 = ((bf16[4,64,8,400]{3,2,0,1:T(8,128)(2,1)}), bf16[4,64,8,400]{3,2,0,1:T(8,128)(2,1)S(1)}, u32[]{:S(2)}, u32[]{:S(2)}) async-start(bf16[4,64,8,400]{3,2,0,1:T(8,128)(2,1)} %copy.356), calls=%async_computation.10 | async-start | bytes 4194304 | tf_op jit(solution)/shard_map/all_to_all | solution.py:303
  472.7 50.9 %all-to-all-done.9 = bf16[4,64,8,400]{3,2,0,1:T(8,128)(2,1)S(1)} async-done(((bf16[4,64,8,400]{3,2,0,1:T(8,128)(2,1)}), bf16[4,64,8,400]{3,2,0,1:T(8,128)(2,1)S(1)}, u32[]{:S(2)}, u32[]{:S(2)}) %all-to-all-start.9) | async-done | bytes 1638432 | tf_op jit(solution)/shard_map/all_to_all | solution.py:303
  532.7 8.4 %fusion.56 = f32[32,16,4,2,48]{4,0,1,2,3:T(8,128)} fusion(f32[4,64,2,16,48]{1,3,2,4,0:T(8,128)S(1)} %bitcast.525, f32[64,1,2,32]{0,3,1,2:T(8,128)S(1)} %copy-done.21, f32[64,1,2,32]{0,3,1,2:T(8,128)S(1)} %copy-done.23), kind=kOutput, calls=%fused_computation.72 | convolution fusion | flops 301998080 | bytes 2392064 | tf_op jit(solution)/shard_map/xypkc,ypqj->jkxqc/dot_general | solution.py:42
  543.8 7.2 %multiply_add_fusion = (f32[8,32,48,48]{3,2,1,0:T(8,128)}, f32[8,32,48,48]{3,2,1,0:T(8,128)}) fusion(f32[8,32,48]{2,1,0:T(8,128)S(1)} %bitcast.550, f32[8,32,48]{2,1,0:T(8,128)S(1)} %bitcast.544, f32[8,32,48]{2,1,0:T(8,128)S(1)} %bitcast.547, f32[8,32,48]{2,1,0:T(8,128)S(1)} %bitcast.541), kind=kLoop, calls=%fused_computation.6 | loop fusion | flops 3538944 | bytes 4915200 | tf_op jit(solution)/shard_map/add | solution.py:117
  571.3 10.9 %all-to-all-start.10 = ((f32[64,1,768]{2,1,0:T(1,128)}), f32[64,1,768]{2,1,0:T(1,128)S(1)}, u32[]{:S(2)}, u32[]{:S(2)}) async-start(f32[64,1,768]{2,1,0:T(1,128)} %reshape.836), calls=%async_computation.12 | async-start | bytes 393216 | tf_op jit(solution)/shard_map/all_to_all | solution.py:130
  (319 shorter events, 237.9 us)
Async XLA Ops:
  7.2 308.0 %copy-start = (bf16[1,48,48]{2,1,0:T(8,128)(2,1)S(1)}, bf16[1,48,48]{2,1,0:T(8,128)(2,1)}, u32[]{:S(2)}) copy-start(bf16[1,48,48]{2,1,0:T(8,128)(2,1)} %param.25) | copy-start | bytes 13828
  7.2 57.9 %reduce-scatter.3.cloned.1.call-start = ((), (), s32[]{:S(2)}) async-start(), calls=%async_computation.13 | async-start | bytes 2621440 | tf_op jit(solution)/shard_map/reduce_scatter | solution.py:177
  13.9 132.2 %copy-start.41 = (bf16[50,16]{0,1:T(8,128)(2,1)}, bf16[50,16]{0,1:T(8,128)(2,1)S(1)}, u32[]{:S(2)}) copy-start(bf16[50,16]{0,1:T(8,128)(2,1)S(1)} %get-tuple-element.58) | copy-start | bytes 4804
  13.9 132.2 %copy-start.43 = (bf16[50,16]{0,1:T(8,128)(2,1)}, bf16[50,16]{0,1:T(8,128)(2,1)S(1)}, u32[]{:S(2)}) copy-start(bf16[50,16]{0,1:T(8,128)(2,1)S(1)} %get-tuple-element.59) | copy-start | bytes 4804
  31.4 61.3 %copy-start.47 = (s32[8]{0:T(128)}, s32[8]{0:T(128)S(1)}, u32[]{:S(2)}) copy-start(s32[8]{0:T(128)S(1)} %and_select_fusion.4) | copy-start | bytes 100
  31.5 58.8 %copy-start.36 = (s32[4,64]{1,0:T(4,128)}, s32[4,64]{1,0:T(4,128)S(1)}, u32[]{:S(2)}) copy-start(s32[4,64]{1,0:T(4,128)S(1)} %iota_add_fusion) | copy-start | bytes 3076
  68.2 21.6 %all-to-all-start = ((f32[64,1,768]{2,1,0:T(1,128)}), f32[64,1,768]{2,1,0:T(1,128)S(1)}, u32[]{:S(2)}, u32[]{:S(2)}) async-start(f32[64,1,768]{2,1,0:T(1,128)} %reshape.824), calls=%async_computation.1 | async-start | bytes 393216 | tf_op jit(solution)/shard_map/all_to_all | solution.py:130
  102.2 16.8 %all-to-all-start.1 = ((f32[64,1,768]{2,1,0:T(1,128)}), f32[64,1,768]{2,1,0:T(1,128)S(1)}, u32[]{:S(2)}, u32[]{:S(2)}) async-start(f32[64,1,768]{2,1,0:T(1,128)} %reshape.826), calls=%async_computation.2 | async-start | bytes 393216 | tf_op jit(solution)/shard_map/all_to_all | solution.py:134
  190.4 58.5 %all-to-all-start.3 = ((bf16[4,64,8,400]{3,2,0,1:T(8,128)(2,1)}), bf16[4,64,8,400]{3,2,0,1:T(8,128)(2,1)S(1)}, u32[]{:S(2)}, u32[]{:S(2)}) async-start(bf16[4,64,8,400]{3,2,0,1:T(8,128)(2,1)} %copy.321), calls=%async_computation.4 | async-start | bytes 4194304 | tf_op jit(solution)/shard_map/all_to_all | solution.py:220
  208.8 40.9 %copy-start.52 = (bf16[1,5,48]{2,1,0:T(8,128)(2,1)S(1)}, bf16[1,5,48]{2,1,0:T(8,128)(2,1)}, u32[]{:S(2)}) copy-start(bf16[1,5,48]{2,1,0:T(8,128)(2,1)} %param.24) | copy-start | bytes 1444
  215.4 116.3 %copy-start.16 = (f32[128,1,2,32]{0,3,2,1:T(8,128)}, f32[128,1,2,32]{0,3,2,1:T(8,128)S(1)}, u32[]{:S(2)}) copy-start(f32[128,1,2,32]{0,3,2,1:T(8,128)S(1)} %get-tuple-element.34) | copy-start | bytes 98308
  215.4 116.3 %copy-start.18 = (f32[128,1,2,32]{0,3,2,1:T(8,128)}, f32[128,1,2,32]{0,3,2,1:T(8,128)S(1)}, u32[]{:S(2)}) copy-start(f32[128,1,2,32]{0,3,2,1:T(8,128)S(1)} %get-tuple-element.43) | copy-start | bytes 98308
  215.5 123.3 %copy-start.31 = (bf16[64,16]{0,1:T(8,128)(2,1)}, bf16[64,16]{0,1:T(8,128)(2,1)S(1)}, u32[]{:S(2)}) copy-start(bf16[64,16]{0,1:T(8,128)(2,1)S(1)} %get-tuple-element.56) | copy-start | bytes 6148
  215.5 123.3 %copy-start.33 = (bf16[64,16]{0,1:T(8,128)(2,1)}, bf16[64,16]{0,1:T(8,128)(2,1)S(1)}, u32[]{:S(2)}) copy-start(bf16[64,16]{0,1:T(8,128)(2,1)S(1)} %get-tuple-element.57) | copy-start | bytes 6148
  258.3 20.6 %all-to-all-start.4 = ((f32[64,1,1536]{2,1,0:T(1,128)}), f32[64,1,1536]{2,1,0:T(1,128)S(1)}, u32[]{:S(2)}, u32[]{:S(2)}) async-start(f32[64,1,1536]{2,1,0:T(1,128)} %reshape.828), calls=%async_computation.5 | async-start | bytes 786432 | tf_op jit(solution)/shard_map/all_to_all | solution.py:130
  307.9 21.7 %all-to-all-start.5 = ((f32[64,1,1536]{2,1,0:T(1,128)}), f32[64,1,1536]{2,1,0:T(1,128)S(1)}, u32[]{:S(2)}, u32[]{:S(2)}) async-start(f32[64,1,1536]{2,1,0:T(1,128)} %reshape.830), calls=%async_computation.6 | async-start | bytes 786432 | tf_op jit(solution)/shard_map/all_to_all | solution.py:134
  346.7 20.8 %all-to-all-start.6 = ((f32[64,1,1536]{2,1,0:T(1,128)}), f32[64,1,1536]{2,1,0:T(1,128)S(1)}, u32[]{:S(2)}, u32[]{:S(2)}) async-start(f32[64,1,1536]{2,1,0:T(1,128)} %reshape.832), calls=%async_computation.7 | async-start | bytes 786432 | tf_op jit(solution)/shard_map/all_to_all | solution.py:130
  402.7 21.2 %all-to-all-start.7 = ((f32[64,1,1536]{2,1,0:T(1,128)}), f32[64,1,1536]{2,1,0:T(1,128)S(1)}, u32[]{:S(2)}, u32[]{:S(2)}) async-start(f32[64,1,1536]{2,1,0:T(1,128)} %reshape.834), calls=%async_computation.8 | async-start | bytes 786432 | tf_op jit(solution)/shard_map/all_to_all | solution.py:134
  465.4 58.2 %copy-start.40 = (pred[4,64,8]{1,2,0:T(8,128)(4,1)S(1)}, pred[4,64,8]{1,2,0:T(8,128)(4,1)}, u32[]{:S(2)}) copy-start(pred[4,64,8]{1,2,0:T(8,128)(4,1)} %copy-done.39) | copy-start | bytes 6148
  465.5 60.8 %copy-start.42 = (bf16[50,16]{0,1:T(8,128)(2,1)S(1)}, bf16[50,16]{0,1:T(8,128)(2,1)}, u32[]{:S(2)}) copy-start(bf16[50,16]{0,1:T(8,128)(2,1)} %copy-done.41) | copy-start | bytes 4804
  465.5 60.8 %copy-start.44 = (bf16[50,16]{0,1:T(8,128)(2,1)S(1)}, bf16[50,16]{0,1:T(8,128)(2,1)}, u32[]{:S(2)}) copy-start(bf16[50,16]{0,1:T(8,128)(2,1)} %copy-done.43) | copy-start | bytes 4804
  465.5 58.1 %all-to-all-start.9 = ((bf16[4,64,8,400]{3,2,0,1:T(8,128)(2,1)}), bf16[4,64,8,400]{3,2,0,1:T(8,128)(2,1)S(1)}, u32[]{:S(2)}, u32[]{:S(2)}) async-start(bf16[4,64,8,400]{3,2,0,1:T(8,128)(2,1)} %copy.356), calls=%async_computation.10 | async-start | bytes 4194304 | tf_op jit(solution)/shard_map/all_to_all | solution.py:303
  472.4 95.8 %reduce-scatter.5.cloned.1.call-start = ((), (), s32[]{:S(2)}) async-start(), calls=%async_computation.14 | async-start | bytes 2621440 | tf_op jit(solution)/shard_map/reduce_scatter | solution.py:177
  571.3 21.8 %all-to-all-start.10 = ((f32[64,1,768]{2,1,0:T(1,128)}), f32[64,1,768]{2,1,0:T(1,128)S(1)}, u32[]{:S(2)}, u32[]{:S(2)}) async-start(f32[64,1,768]{2,1,0:T(1,128)} %reshape.836), calls=%async_computation.12 | async-start | bytes 393216 | tf_op jit(solution)/shard_map/all_to_all | solution.py:130
  (50 other events, 389.9 us)
Sparse Core Ops, SparseCore 0:
  29.0 36.0 reduce-scatter.2
  541.3 26.8 reduce-scatter.4
where the time goes:
time: 621 us; the launch traced here: 610 us
  waiting for transfers between devices  180 us (29%)
  matrix products  131 us (21%)
  local copies, waits for them, and re-layouts  109 us (18%)
  blocking collectives  77.3 us (12%)
  starting transfers between devices  68 us (11%)
  other arithmetic  28.1 us (5%)
  between operations  16.6 us (3%)
    all_to_all x1, waiting for transfers between devices, shards(): lax.all_to_all(lax.all_to_all(outgoing.astype(jnp.bfloat16), 'level', spl...  50.9 us
    reduce_scatter x2, waiting for transfers between devices, coarse_forward(): lax.psum_scatter(along_y(spectra, cosine, sine_part), 'level', scatter_di...  38.6 us
    all_to_all x4, starting transfers between devices, to_modes(): lax.all_to_all(blocks, 'wide', split_axis=0, concat_axis=1, tiled=True)  33.8 us
    all_to_all x1, waiting for transfers between devices, shards(): lax.all_to_all(lax.all_to_all(outgoing, 'level', split_axis=0, concat_axi...  33.4 us
    unnamed x146, local copies, waits for them, and re-layouts  32.1 us
    all_to_all x3, waiting for transfers between devices, from_modes(): lax.all_to_all(back_x(spectra, length), 'wide', split_axis=1, concat_axis...  30.9 us
    all_to_all x1, blocking collectives, shards(): lax.all_to_all(outgoing.astype(jnp.bfloat16), 'level', split_axis=0, conc...  28.5 us
    all_to_all x1, blocking collectives, shards(): lax.all_to_all(outgoing, 'level', split_axis=0, concat_axis=0, tiled=True)  27.8 us
  transfers between devices with their start and end apart: 11, of which 11 were waited for; matrix products, arithmetic and copies ran while one was open for 12% of the time, Pallas kernels for 0%

commit v1 on v0

v1 whole, which is shorter than its diff:
```python
import math

import ml_dtypes
import numpy as np
import jax
import jax.numpy as jnp
from jax import lax
from jax.experimental import pallas as pl
from jax.experimental.pallas import tpu as pltpu
from jax.sharding import PartitionSpec as P

MODES = 16
KF = 2 * MODES
CH = 48
NB = 6
CL = 8
GX = 256
GY = 256
GZ = 50
FX = 128
FY = 128
FZ = 64
ZP = 64
LV = 4
WD = 64
PG = 4
YG = 64
PF = 2
CC = CH * CH
BF = jnp.bfloat16
F32 = jnp.float32
HIGH = lax.Precision.HIGHEST
VMEM_BYTES = 48 * 2**20


def bf(x):
    return np.asarray(x, np.float32).astype(ml_dtypes.bfloat16)


def f32(x):
    return np.asarray(x, np.float32)


def waves(rows, length):
    j = np.arange(KF)
    signed = np.where(j < MODES, j, j - KF)
    turn = np.mod(rows[:, None] * signed[None, :], length) * (2.0 * math.pi / length)
    return np.cos(turn) / math.sqrt(length), np.sin(turn) / math.sqrt(length)


def forward_table(rows, length):
    c, s = waves(rows, length)
    c, s = c.T, s.T
    return np.stack([np.stack([c, s], 1), np.stack([-s, c], 1)], 0)


def depth(length):
    c, s = waves(np.arange(length), length)
    both = np.stack([c[:, :MODES], -s[:, :MODES]], 1)
    both = bf(both).astype(np.float64)
    return np.concatenate([both, np.zeros((ZP - length, 2, MODES))], 0)


D_G, D_F = depth(GZ), depth(FZ)
ZMAP = np.zeros((ZP, FZ))
ZMAP[np.arange(FZ) * GZ // FZ, np.arange(FZ)] = 1.0
D_POOL = np.einsum("gf,frk->grk", ZMAP, D_F)


def depth_blocks(d):
    return np.einsum("zrk,ij->zirkj", d, np.eye(CL)).reshape(ZP * CL, 2 * MODES * CL)


def depth_features(d, length):
    return np.einsum("zrk,ij->zirkj", d[:length], np.eye(4)).reshape(length * 4, 2 * MODES * 4)


ZF_G, ZF_F = bf(depth_blocks(D_G)), bf(depth_blocks(D_F))
ZI_G, ZI_F = bf(depth_blocks(D_G).T), bf(depth_blocks(D_F).T)
Z4_G, Z4_F = bf(depth_features(D_G, GZ)), bf(depth_features(D_F, FZ))
ZC = f32(D_POOL.reshape(ZP, 2 * MODES))

FY_G = np.stack([forward_table(v * YG + np.arange(YG), GY) for v in range(LV)], 0)
FY_F = forward_table(np.arange(FY), FY)
FY_BOX = FY_F.reshape(2, KF, 2, FY // 2, 2).sum(4)
FX_G = forward_table(np.arange(GX), GX)
FX_F = forward_table(np.arange(FX), FX)
FX_BOX = FX_F.reshape(2, KF, 2, FX // 2, 2).sum(4)
EYE_G, EYE_F = np.eye(PG), np.eye(PF)

TYA_G = f32(np.einsum("vakbt,pq->vakpbtq", FY_G, EYE_G).reshape(LV, 2 * KF * PG, 2 * YG * PG))
TYA_F = f32(np.einsum("akbt,pq->akpbtq", FY_F, EYE_F).reshape(2 * KF * PF, 2 * FY * PF))
TYA_BOX = f32(np.einsum("akbt,pq->akpbtq", FY_BOX, EYE_G).reshape(2 * KF * PG, FY * PG))
TYF_G = bf(np.einsum("vakbt,pq->vkpabtq", FY_G, EYE_G).reshape(LV, KF * PG * 2, 2 * YG * PG))
TYF_F = bf(np.einsum("akbt,pq->kpabtq", FY_F, EYE_F).reshape(KF * PF * 2, 2 * FY * PF))
TYI_G = bf(np.einsum("vbkat,pq->vatpkqb", FY_G, EYE_G).reshape(LV, 2 * YG * PG, KF * PG * 2))
TYI_F = bf(np.einsum("bkat,pq->atpkqb", FY_F, EYE_F).reshape(2 * FY * PF, KF * PF * 2))
TYB_BOX = np.zeros((4, 448, 2 * KF), np.float32)
TYB_BOX[:, 192:256] = np.repeat(FY_BOX.transpose(2, 0, 3, 1).reshape(4, FY // 2, KF), 2, axis=2)
DD_BOX = bf(np.einsum("zahk,pq,rs->hprkasqz", D_POOL.reshape(ZP, 2, 2, 8), EYE_G, np.eye(2)).reshape(128, 4 * PG * ZP))


def source_rows(table):
    a = np.stack([table[0], -table[1]], 1)
    b = np.stack([table[1], table[0]], 1)
    return np.stack([a, b], 0).reshape(4 * KF, 2, -1)


def in_rows(table, planes, first):
    rows = source_rows(table).reshape(4 * KF, 2, WD, planes)
    out = np.zeros((4 * KF, 2, WD, 8))
    out[..., first : first + planes] = rows
    return out.reshape(4 * KF, 2 * WD * 8)


TXS_G = f32(in_rows(FX_G, PG, 0))
TXS_F = f32(in_rows(FX_F, PF, PG))
TXS_BOX = f32(source_rows(FX_BOX).reshape(4 * KF, FX))


def dual_rows(table, count):
    r, i = table[0], table[1]
    kinds = [np.stack([r, r], 1), np.stack([i, i], 1), np.stack([r, i], 1), np.stack([i, -r], 1)]
    rows = np.stack(kinds[:count], 0).transpose(0, 1, 2, 4, 3)
    return rows.reshape(count * 2 * KF, -1)


TXD_G = bf(dual_rows(FX_G, 2))
TXD_F = bf(dual_rows(FX_F, 4))


def back_rows(table):
    back = table.transpose(3, 2, 0, 1)
    back = np.stack([back, back], 4)
    return back.reshape(back.shape[0] * 2, 4 * KF)


TXB_G = bf(back_rows(FX_G))
TXB_F = bf(back_rows(FX_F))
TXB_BOX = f32(back_rows(FX_BOX))

PERM = np.zeros((MODES, NB, CL, NB, MODES, CL))
for _k in range(MODES):
    for _b in range(NB):
        for _l in range(CL):
            PERM[_k, _b, _l, _b, _k, _l] = 1.0
PERM = PERM.reshape(MODES * CH, MODES * CH)
PERM_IN, PERM_OUT = bf(PERM), bf(PERM.T)
PERM_WIDE = np.zeros((8, 128, MODES * CH))
PERM_WIDE[:, : 2 * CH] = PERM.reshape(8, 2 * CH, MODES * CH)
PERM_WIDE = bf(PERM_WIDE.reshape(1024, MODES * CH))
SPREAD_IN = bf(np.kron(np.eye(CH), np.ones((1, CH))))
SPREAD_OUT = bf(np.kron(np.ones((1, CH)), np.eye(CH)))
FOLD_IN = bf(np.kron(np.ones((CH, 1)), np.eye(CH)))
ONES_CL = bf(np.kron(np.eye(ZP), np.ones((1, CL))))
SUM_CL = bf(np.kron(np.eye(ZP), np.ones((CL, 1))))
TILE_CL = f32(np.kron(np.ones((1, ZP)), np.eye(CL)))
ROWS_UP = np.kron(np.eye(FY // 2), np.ones((2 * PF, 1))).reshape(256, FY // 4, 2).transpose(2, 0, 1)
ROWS_UP = bf(ROWS_UP)
ROWS_DOWN = f32(np.kron(np.eye(FY // 2), np.ones((1, 2 * PF))))
Z_UP = bf(ZMAP)
Z_DOWN = f32(ZMAP.T)


def mm(a, b):
    return jnp.dot(a, b, preferred_element_type=F32)


def mmh(a, b):
    return jnp.dot(a, b, preferred_element_type=F32, precision=HIGH)


MESH = pl.DeviceIdType.MESH
DMA2 = pltpu.SemaphoreType.DMA((2,))


def vm(shape, kind=F32):
    return pltpu.VMEM(shape, kind)


def run(body, outs, *args, meta=None, scratch=(), cid=None, name=None):
    specs = [pl.BlockSpec(memory_space=pltpu.VMEM)] * len(args)
    if meta is not None:
        specs = [pl.BlockSpec(memory_space=pltpu.SMEM)] + specs
        args = (meta,) + args
    return pl.pallas_call(
        body,
        out_shape=[jax.ShapeDtypeStruct(s, d) for s, d in outs],
        in_specs=specs,
        out_specs=[pl.BlockSpec(memory_space=pltpu.VMEM)] * len(outs),
        scratch_shapes=list(scratch),
        name=name,
        compiler_params=pltpu.CompilerParams(
            vmem_limit_bytes=VMEM_BYTES, collective_id=cid, has_side_effects=cid is not None),
    )(*args)


def features_body(rows, planes, width, x_ref, z_ref, t_ref, feat_ref, out_ref, scr, level=None):
    for y in range(rows):
        scr[planes * y : planes * (y + 1), :] = x_ref[:, width * y : width * (y + 1)].astype(F32)
    feat = scr[...].astype(BF)
    feat_ref[...] = feat
    a = mm(feat, z_ref[...])
    half = a.shape[1] // 2
    stacked = jnp.concatenate([a[:, :half], a[:, half:]], axis=0)
    both = mmh(t_ref[...] if level is None else t_ref[level], stacked)
    rows_out = both.shape[0] // 2
    lanes = jnp.concatenate([both[:rows_out], both[rows_out:]], axis=1)
    out_ref[...] = lanes.reshape(out_ref.shape)


def features_g_body(meta, x_ref, z_ref, t_ref, feat_ref, out_ref, scr):
    features_body(YG, PG, GZ * 4, x_ref, z_ref, t_ref, feat_ref, out_ref, scr, meta[0])


def features_f_body(x_ref, z_ref, t_ref, feat_ref, out_ref, scr):
    features_body(FY, PF, FZ * 4, x_ref, z_ref, t_ref, feat_ref, out_ref, scr)


def pair_rows(scr, first, stride, count):
    even = scr[pl.ds(first, count, stride=2 * stride), :]
    odd = scr[pl.ds(first + stride, count, stride=2 * stride), :]
    return jnp.concatenate([even, odd], axis=1)


def box_body(meta, rows_ref, z_ref, t_ref, spec_ref, planes_ref, rows_scr, box_scr, s_scr, o_scr):
    rows_scr[...] = rows_ref[...].astype(F32).reshape(rows_scr.shape)
    box = rows_scr[pl.ds(pl.multiple_of(meta[2] * PG, 32), 256), :]
    box_scr[...] = box
    for p in range(PG):
        planes_ref[lax.rem(p + GX - meta[1], PG)] = pair_rows(box_scr, p, PG, FY // 4).astype(BF)
    a = mmh(box, z_ref[...])
    s_scr[...] = mmh(t_ref[...], jnp.concatenate([a[:, :MODES], a[:, MODES:]], axis=0))
    for p in range(PG):
        for r in range(2):
            at = 2 * MODES * p + MODES * r
            o_scr[:, at : at + MODES] = s_scr[pl.ds(KF * PG * r + p, KF, stride=PG), :]
    spec_ref[...] = o_scr[...].reshape(spec_ref.shape)


def mix_modes(s, modes, w_ref, e_ref, r_ref, t_ref, put, extra=None):
    half = s.shape[0] // 2
    for m in range(modes):
        sa = s[:half, CH * m : CH * (m + 1)].astype(BF)
        sb = s[half:, CH * m : CH * (m + 1)].astype(BF)
        w = w_ref[m].reshape(half, CC).astype(F32)
        pa = mm((w * mm(sa, e_ref[...])).astype(BF), r_ref[...])
        pb = mm((w * mm(sb, e_ref[...])).astype(BF), r_ref[...])
        both = jnp.concatenate([pa, pb], axis=0).astype(BF)
        put(m, mm(t_ref[...], both))
        if extra is not None:
            extra(m, w)


def halves(u):
    half = u.shape[1] // 2
    return jnp.concatenate([u[:, :half], u[:, half:]], axis=0)


def selector(lift_ref, count, first):
    rows = lax.broadcasted_iota(jnp.int32, (MODES * 4, count * CH), 0)
    cols = lax.broadcasted_iota(jnp.int32, (MODES * 4, count * CH), 1)
    tiled = jnp.concatenate([lift_ref[:4, :].astype(F32)] * MODES, axis=0)
    tiled = jnp.concatenate([tiled] * count, axis=1)
    mode = sum((cols >= CH * m).astype(jnp.int32) for m in range(1, count))
    return jnp.where(lax.shift_right_logical(rows, 2) == first + mode, tiled, 0.0)


def selector_last(lift_ref, count, first):
    rows = lax.broadcasted_iota(jnp.int32, (MODES, count * CH), 0)
    cols = lax.broadcasted_iota(jnp.int32, (MODES, count * CH), 1)
    tiled = jnp.concatenate([lift_ref[4:5, :].astype(F32)] * count, axis=1)
    mode = sum((cols >= CH * m).astype(jnp.int32) for m in range(1, count))
    return jnp.where(rows == first + mode, tiled, 0.0)


def mix_g_body(meta, u_ref, tx_ref, l_ref, w_ref, e_ref, r_ref, tb_ref, s_ref, p_ref, p_scr):
    u = u_ref[...].reshape(WD * 8, 128)
    s = mmh(mmh(tx_ref[...], halves(u)), selector(l_ref, 2, 2 * lax.rem(meta[3], 8)))
    s_ref[...] = s
    p_scr[...] = jnp.zeros(p_scr.shape, F32)

    def put(m, value):
        p_scr[:, CH * m : CH * (m + 1)] = value

    mix_modes(s, 2, w_ref, e_ref, r_ref, tb_ref, put)
    p_ref[...] = p_scr[...].reshape(p_ref.shape)


def mix_f_body(meta, u_ref, tx_ref, l_ref, c_ref, txc_ref, w_ref, e_ref, r_ref, tb_ref, s_ref, p_ref, v_ref, x_scr, p_scr):
    first = 8 * lax.rem(meta[3], 2)
    u = u_ref[...].reshape(WD * 8, 128)
    s = mmh(mmh(tx_ref[...], halves(u)), selector(l_ref, 8, first))
    got = c_ref[...].reshape(WD, 128)
    for p in range(PG):
        x_scr[pl.ds(p, WD, stride=PG), :] = got[:, 2 * MODES * p : 2 * MODES * (p + 1)]
    box = x_scr[pl.ds(meta[1], FX // 2), :]
    s = s + mmh(mmh(txc_ref[...], halves(box)), selector_last(l_ref, 8, first))
    s_ref[...] = s
    lift_lanes = mm(l_ref[...], e_ref[...])[4:5, :]

    def put(m, value):
        p_scr[:, CH * m : CH * (m + 1)] = value

    def extra(m, w):
        v_ref[2 * KF * m : 2 * KF * (m + 1), :] = mm((w * lift_lanes).astype(BF), r_ref[...])

    mix_modes(s, 8, w_ref, e_ref, r_ref, tb_ref, put, extra)
    p_ref[...] = p_scr[...].reshape(p_ref.shape)


K0 = math.sqrt(2.0 / math.pi)


def gelu_parts(x):
    x2 = x * x
    t = jnp.tanh(K0 * x * (1.0 + 0.044715 * x2))
    hidden = 0.5 * x * (1.0 + t)
    slope = 0.5 * (1.0 + t) + 0.5 * x * (1.0 - t * t) * (K0 * (1.0 + 3.0 * 0.044715 * x2))
    return hidden, slope


def block_pre(bb, b, zi_ref):
    rows = bb.shape[0] // 2
    lanes = slice(MODES * CL * b, MODES * CL * (b + 1))
    return mm(bb[:rows, lanes], zi_ref[: MODES * CL]) + mm(bb[rows:, lanes], zi_ref[MODES * CL :])


def lanes_of(row, b, tile_ref):
    return mmh(row[:, CL * b : CL * (b + 1)], tile_ref[...])


def point_block(point, b, tile_ref, rows):
    lanes = lanes_of(point, b, tile_ref)
    full = jnp.concatenate([lanes] * (rows // 4), axis=0)
    z_row = lax.shift_right_logical(lax.broadcasted_iota(jnp.int32, full.shape, 0), 2)
    z_col = lax.shift_right_logical(lax.broadcasted_iota(jnp.int32, full.shape, 1), 3)
    return jnp.where(z_row == z_col, full, 0.0).astype(BF)


def split(x):
    top = x.astype(BF)
    return top, (x - top.astype(F32)).astype(BF)


def mm_split(x, table):
    top, low = split(x)
    return mm(top, table) + mm(low, table)


def field_g_body(meta, x_ref, perm_ref, ty_ref, zi_ref, feat_ref, lift_ref, mix_ref, ro_ref, tile_ref, sum_ref,
                 pred_ref, slope_ref, f_scr, x_scr, acc):
    f_scr[...] = x_ref[...].astype(F32).reshape(f_scr.shape)
    for q in range(8):
        x_scr[:, 128 * q : 128 * (q + 1)] = f_scr[:, q].reshape(256, 128).astype(BF)
    bb = mm(ty_ref[meta[0]], mm(x_scr[...], perm_ref[...]).astype(BF)).astype(BF)
    point = mmh(lift_ref[...].astype(F32), mix_ref[...].astype(F32))
    readout = ro_ref[...].astype(F32)
    for b in range(NB):
        pre = block_pre(bb, b, zi_ref) + mm(feat_ref[...], point_block(point, b, tile_ref, GZ * 4))
        hidden, slope = gelu_parts(pre)
        slope_ref[b] = slope.astype(BF)
        part = hidden * lanes_of(readout, b, tile_ref)
        if b == 0:
            acc[...] = part
        else:
            acc[...] += part
    pred_ref[...] = mm_split(acc[...], sum_ref[...]).astype(BF)


def put_block(a_scr, gp, b, zf_ref):
    a = mm(gp, zf_ref[...]).astype(BF)
    rows = a.shape[0]
    width = MODES * CL
    a_scr[:rows, width * b : width * (b + 1)] = a[:, :width]
    a_scr[rows:, width * b : width * (b + 1)] = a[:, width:]


def forward_tail(a_scr, table, perm_ref):
    return mm(mm(table, a_scr[...]).astype(BF), perm_ref[...])


def field_f_body(meta, x_ref, perm_ref, ty_ref, zi_ref, feat_ref, lift_ref, mix_ref, ro_ref, tile_ref, sum_ref,
                 box_ref, zup_ref, rup_ref, cot_ref, ones_ref, zf_ref, tyf_ref, permo_ref, rdn_ref, zdn_ref,
                 pred_ref, send_ref, pt_ref, x_scr, cot_scr, a_scr, acc, acc_pt, pt_scr):
    for h in range(2):
        x_scr[:, 8 * CH * h : 8 * CH * (h + 1)] = x_ref[:, h].reshape(128, 8 * CH).astype(BF)
    bb = mm(ty_ref[...], mm(x_scr[...], perm_ref[...]).astype(BF)).astype(BF)
    for y in range(FY):
        cot_scr[PF * y : PF * (y + 1), :] = cot_ref[:, FZ * y : FZ * (y + 1)]
    wide_cot = mm_split(cot_scr[...], ones_ref[...])
    plane = box_ref[lax.div(meta[1] + meta[3], PG)]
    rows = mm(rup_ref[0], plane[:, :ZP]) + mm(rup_ref[1], plane[:, ZP:])
    cl = mm(rows.astype(BF), zup_ref[...]).astype(BF)
    point = mmh(lift_ref[...].astype(F32), mix_ref[...].astype(F32))
    readout = ro_ref[...].astype(F32)
    for b in range(NB):
        lc = jnp.concatenate([lanes_of(point[4:5], b, tile_ref)] * ZP, axis=0)
        z_row = lax.broadcasted_iota(jnp.int32, lc.shape, 0)
        z_col = lax.shift_right_logical(lax.broadcasted_iota(jnp.int32, lc.shape, 1), 3)
        lc = jnp.where(z_row == z_col, lc, 0.0).astype(BF)
        pre = block_pre(bb, b, zi_ref) + mm(feat_ref[...], point_block(point[:4], b, tile_ref, FZ * 4)) + mm(cl, lc)
        hidden, slope = gelu_parts(pre)
        ro_lanes = lanes_of(readout, b, tile_ref)
        gp = (slope * (wide_cot * ro_lanes)).astype(BF)
        part = hidden * ro_lanes
        part_pt = gp.astype(F32) * lanes_of(point[4:5], b, tile_ref)
        if b == 0:
            acc[...] = part
            acc_pt[...] = part_pt
        else:
            acc[...] += part
            acc_pt[...] += part_pt
        put_block(a_scr, gp, b, zf_ref)
    pred_ref[...] = mm_split(acc[...], sum_ref[...]).astype(BF)
    z = forward_tail(a_scr, tyf_ref[...], permo_ref)
    for h in range(2):
        send_ref[:, h] = z[:, 8 * CH * h : 8 * CH * (h + 1)].reshape(KF, 2 * PF, 8 * CH)
    pt_scr[...] = mmh(mmh(rdn_ref[...], mm_split(acc_pt[...], sum_ref[...])), zdn_ref[...])
    pt_ref[...] = pair_rows(pt_scr, 0, 1, FY // 4).astype(BF)


def dual_f_body(meta, z_ref, tx_ref, v_ref, tb_ref, pt_ref, dual_ref, q_ref, mine_ref, q_scr, o_scr):
    z = mm(tx_ref[...], z_ref[...].reshape(2 * FX, 8 * CH).astype(BF))
    rows = 2 * KF
    dual_ref[...] = z[: 2 * rows].astype(BF)
    zc, zd = z[2 * rows : 3 * rows], z[3 * rows :]
    cols = []
    for m in range(8):
        v = v_ref[rows * m : rows * (m + 1), :]
        lanes = slice(CH * m, CH * (m + 1))
        cols.append(jnp.concatenate([
            jnp.sum(v * zc[:, lanes], axis=1, keepdims=True),
            jnp.sum(v * zd[:, lanes], axis=1, keepdims=True)], axis=0))
    q_scr[...] = jnp.zeros(q_scr.shape, F32)
    q_scr[2 * GX : 2 * GX + FX, :] = mmh(tb_ref[...], jnp.concatenate(cols, axis=1))
    o_scr[: 2 * GX, :] = q_scr[pl.ds(2 * GX - 2 * meta[1], 2 * GX), :]
    lanes = [o_scr[pl.ds(r, WD, stride=8), :] for r in range(8)]
    lanes.append(jnp.zeros((WD, 64), F32))
    q_ref[...] = jnp.concatenate(lanes, axis=1).reshape(q_ref.shape)
    for p in range(PG):
        at = PG * meta[3] + p - meta[1]
        ok = jnp.logical_and(at >= 0, at < WD)
        plane = pt_ref[jnp.clip(at, 0, WD - 1)]
        mine_ref[32 * p : 32 * (p + 1), :] = jnp.where(ok, plane, jnp.zeros_like(plane))


def grad_modes(modes, s_ref, d_ref, e_ref, o_ref, g_ref):
    rows = 2 * KF
    for m in range(modes):
        lanes = slice(CH * m, CH * (m + 1))
        sa = mm(s_ref[:rows, lanes].astype(BF), e_ref[...])
        sb = mm(s_ref[rows:, lanes].astype(BF), e_ref[...])
        za = mm(d_ref[:rows, lanes], o_ref[...])
        zb = mm(d_ref[rows:, lanes], o_ref[...])
        g_ref[m] = (sa * za + sb * zb).reshape(KF, 2, CC)


def grad_f_body(s_ref, d_ref, e_ref, o_ref, g_ref):
    grad_modes(8, s_ref, d_ref, e_ref, o_ref, g_ref)


def dual_g_body(z_ref, tx_ref, s_ref, e_ref, o_ref, g_ref, d_scr):
    z = z_ref[...].reshape(2 * GX, 128)[:, : 2 * CH]
    d_scr[...] = mm(tx_ref[...], z.astype(BF)).astype(BF)
    grad_modes(2, s_ref, d_scr, e_ref, o_ref, g_ref)


def back_g_body(meta, q_ref, dd_ref, ty_ref, pt_ref, cot_ref, slope_ref, ro_ref, tile_ref, ones_ref, zf_ref, tyf_ref,
                permo_ref, send_ref, cot_scr, pad_scr, a_scr):
    level = meta[0]
    cot_scr[...] = jnp.zeros(cot_scr.shape, F32)
    for y in range(YG):
        cot_scr[PG * y : PG * (y + 1), :GZ] = cot_ref[:, GZ * y : GZ * (y + 1)]
    q = q_ref[...].reshape(LV * WD, 128)[:, :64]
    odd = jnp.bitwise_and(lax.broadcasted_iota(jnp.int32, q.shape, 0), 1) == 1
    q = jnp.concatenate([jnp.where(odd, 0.0, q), jnp.where(odd, q, 0.0)], axis=1).astype(BF)
    g = mm(q, dd_ref[...]).astype(BF)
    total = jnp.zeros((YG, PG * ZP), F32)
    for l in range(LV):
        start = pl.multiple_of(192 + YG * level - meta[4 + l], 8)
        for k in range(4):
            t = ty_ref[k, pl.ds(start, YG), :].astype(BF)
            total += mm(t, g[WD * l : WD * (l + 1), PG * ZP * k : PG * ZP * (k + 1)])
    for p in range(PG):
        cot_scr[pl.ds(p, YG, stride=PG), :] += total[:, ZP * p : ZP * (p + 1)]
    pad_scr[...] = jnp.zeros(pad_scr.shape, F32)
    planes = [jnp.zeros((32, 128), F32) for _ in range(PG)]
    for l in range(LV):
        start = 96 + 32 * level - lax.div(meta[4 + l], 2)
        for p in range(PG):
            pad_scr[l, p, 96:128, :] = pt_ref[l, 32 * p : 32 * (p + 1), :].astype(F32)
            planes[p] += pad_scr[l, p, pl.ds(start, 32), :]
    for p in range(PG):
        for k in range(2):
            cot_scr[pl.ds(PG * k + p, 32, stride=2 * PG), :] += planes[p][:, ZP * k : ZP * (k + 1)]
    wide_cot = mm_split(cot_scr[...], ones_ref[...])
    readout = ro_ref[...].astype(F32)
    for b in range(NB):
        gp = (slope_ref[b].astype(F32) * (wide_cot * lanes_of(readout, b, tile_ref))).astype(BF)
        put_block(a_scr, gp, b, zf_ref)
    send_ref[...] = forward_tail(a_scr, tyf_ref[level], permo_ref).astype(BF).reshape(send_ref.shape)


def here():
    return lax.axis_index("level"), lax.axis_index("wide")


def greet(with_level, with_wide):
    level, wide = here()
    barrier = pltpu.get_barrier_semaphore()
    count = 0
    if with_level:
        for i in range(1, LV):
            pl.semaphore_signal(barrier, inc=1, device_id=(lax.rem(level + i, LV), wide), device_id_type=MESH)
        count += LV - 1
    if with_wide:
        def one(i, carry):
            pl.semaphore_signal(barrier, inc=1, device_id=(level, lax.rem(wide + i, WD)), device_id_type=MESH)
            return carry

        lax.fori_loop(1, WD, one, 0)
        count += WD - 1
    return barrier, count


def remote(src, dst, sems, to):
    return pltpu.make_async_remote_copy(
        src_ref=src, dst_ref=dst, send_sem=sems.at[0], recv_sem=sems.at[1], device_id=to, device_id_type=MESH)


def push_wide(pairs):
    level, wide = here()

    def one(i, carry):
        peer = lax.rem(wide + i, WD)
        for source, land, sems in pairs:
            remote(source(peer), land.at[wide], sems, (level, peer)).start()
        return carry

    lax.fori_loop(1, WD, one, 0)


def push_level(source, land, sems):
    level, wide = here()
    for i in range(1, LV):
        peer = lax.rem(level + i, LV)
        remote(source(peer), land.at[level], sems, (peer, wide)).start()


def finish(land, sems, count):
    level, wide = here()
    part = land.at[pl.ds(0, count - 1)]
    done = remote(part, part, sems, (level, wide))
    done.wait_send()
    done.wait_recv()


def exchange_in_body(kg_ref, kf_ref, out_ref, land, msg, s_level, s_wide):
    level, wide = here()
    barrier, count = greet(True, True)
    msg[...] = jnp.zeros(msg.shape, F32)
    for w in range(WD):
        msg[w, PG : PG + PF, :] = kf_ref[w // 2]
    land[level] = kg_ref[pl.ds(8 * level, 8)]
    pl.semaphore_wait(barrier, count)
    push_level(lambda peer: kg_ref.at[pl.ds(8 * peer, 8)], land, s_level)
    finish(land, s_level, LV)
    total = land[0] + land[1] + land[2] + land[3]
    for w in range(WD):
        msg[w, :PG, :] = total[w // 8]
    push_wide([(lambda peer: msg.at[peer], out_ref, s_wide)])
    out_ref[wide] = msg[wide]
    finish(out_ref, s_wide, WD)


def exchange_g_body(p_ref, out_ref, land, s_wide, s_level):
    level, wide = here()
    barrier, count = greet(True, True)
    land[wide] = p_ref[wide]
    pl.semaphore_wait(barrier, count)
    push_wide([(lambda peer: p_ref.at[peer], land, s_wide)])
    finish(land, s_wide, WD)
    out_ref[level] = land[...].reshape(WD * 8, 128).astype(BF)
    push_level(lambda peer: out_ref.at[level], out_ref, s_level)
    finish(out_ref, s_level, LV)


def gather_level_body(x_ref, out_ref, s_level):
    level, wide = here()
    barrier, count = greet(True, False)
    out_ref[level] = x_ref[...]
    pl.semaphore_wait(barrier, count)
    push_level(lambda peer: x_ref, out_ref, s_level)
    finish(out_ref, s_level, LV)


def exchange_box_body(spec_ref, planes_ref, got_ref, box_ref, s_spec, s_box):
    level, wide = here()
    barrier, count = greet(False, True)
    got_ref[wide] = spec_ref[wide // 2]
    box_ref[wide] = planes_ref[wide % PG]
    pl.semaphore_wait(barrier, count)
    push_wide([(lambda peer: spec_ref.at[peer // 2], got_ref, s_spec),
               (lambda peer: planes_ref.at[peer % PG], box_ref, s_box)])
    finish(got_ref, s_spec, WD)
    finish(box_ref, s_box, WD)


def exchange_f_body(x_ref, out_ref, s_wide):
    level, wide = here()
    barrier, count = greet(False, True)
    out_ref[wide] = x_ref[wide]
    pl.semaphore_wait(barrier, count)
    push_wide([(lambda peer: x_ref.at[peer], out_ref, s_wide)])
    finish(out_ref, s_wide, WD)


def exchange_dual_body(x_ref, pt_ref, out_ref, all_ref, s_wide, s_pt):
    level, wide = here()
    barrier, count = greet(False, True)
    out_ref[wide] = x_ref[wide]
    all_ref[wide] = pt_ref[...]
    pl.semaphore_wait(barrier, count)
    push_wide([(lambda peer: x_ref.at[peer], out_ref, s_wide), (lambda peer: pt_ref, all_ref, s_pt)])
    finish(out_ref, s_wide, WD)
    finish(all_ref, s_pt, WD)


def exchange_back_body(q_ref, pt_ref, out_ref, pts_ref, s_wide, s_level, s_pt):
    level, wide = here()
    barrier, count = greet(True, True)
    own = out_ref.at[level]
    own[wide] = q_ref[wide]
    pts_ref[level] = pt_ref[...]
    pl.semaphore_wait(barrier, count)
    push_level(lambda peer: pt_ref, pts_ref, s_pt)
    push_wide([(lambda peer: q_ref.at[peer], own, s_wide)])
    finish(own, s_wide, WD)
    push_level(lambda peer: out_ref.at[level], out_ref, s_level)
    finish(out_ref, s_level, LV)
    finish(pts_ref, s_pt, LV)


def exchange_out_body(x_ref, out_ref, land, msg, s_level, s_wide):
    level, wide = here()
    barrier, count = greet(True, True)
    msg[...] = jnp.zeros(msg.shape, F32)
    land[level] = x_ref[level]
    pl.semaphore_wait(barrier, count)
    push_level(lambda peer: x_ref.at[peer], land, s_level)
    finish(land, s_level, LV)
    total = land[0].astype(F32) + land[1].astype(F32) + land[2].astype(F32) + land[3].astype(F32)
    for q in range(8):
        msg[:, q, :, : 2 * CH] = total[:, 2 * CH * q : 2 * CH * (q + 1)].reshape(8, 8, 2 * CH)
    push_wide([(lambda peer: msg.at[peer // 8, peer % 8], out_ref, s_wide)])
    out_ref[wide] = msg[wide // 8, wide % 8]
    finish(out_ref, s_wide, WD)


def shards(coarse_input, fine_input, coarse_cotangent, fine_cotangent, well_x, well_y, coarse_lift, coarse_mixing,
           coarse_spectral, coarse_readout, fine_lift, fine_mixing, fine_spectral, fine_readout):
    level = lax.axis_index("level")
    wide = lax.axis_index("wide")
    meta = jnp.concatenate([
        jnp.stack([level, well_x[level], 8 * well_y[level], wide]).astype(jnp.int32), 8 * well_y])
    row_g, row_f = coarse_readout[None], fine_readout
    lift_f, mixing_f = fine_lift[0], fine_mixing[0]

    feat_g, kg = run(features_g_body, [((256, GZ * 4), BF), ((KF, PG, 128), F32)],
                     coarse_input, Z4_G, TYA_G, meta=meta, scratch=[vm((256, GZ * 4))], name="features_g")
    feat_f, kf = run(features_f_body, [((256, FZ * 4), BF), ((KF, PF, 128), F32)],
                     fine_input[0], Z4_F, TYA_F, scratch=[vm((256, FZ * 4))], name="features_f")
    (got_in,) = run(exchange_in_body, [((WD, 8, 128), F32)], kg, kf,
                    scratch=[vm((LV, 8, PG, 128)), vm((WD, 8, 128)), DMA2, DMA2], cid=1, name="exchange_in")
    s_g, p_g = run(mix_g_body, [((4 * KF, 2 * CH), F32), ((WD, 8, 128), F32)],
                   got_in, TXS_G, coarse_lift, coarse_spectral, SPREAD_IN, FOLD_IN, TXB_G, meta=meta,
                   scratch=[vm((2 * GX, 128))], name="mix_g")
    (x_g,) = run(exchange_g_body, [((LV, WD * 8, 128), BF)], p_g,
                 scratch=[vm((WD, 8, 128)), DMA2, DMA2], cid=2, name="exchange_g")
    pred_g, slope_g = run(
        field_g_body, [((256, ZP), BF), ((NB, 256, ZP * CL), BF)],
        x_g, PERM_WIDE, TYI_G, ZI_G, feat_g, coarse_lift, coarse_mixing, row_g, TILE_CL, SUM_CL, meta=meta,
        scratch=[vm((KF, 8, 8, 128)), vm((256, 1024), BF), vm((256, ZP * CL))], name="field_g")
    (rows_all,) = run(gather_level_body, [((LV, 256, ZP), BF)], pred_g, scratch=[DMA2], cid=3, name="gather_rows")
    spec_c, planes_c = run(
        box_body, [((KF, 1, 128), F32), ((PG, 32, 128), BF)], rows_all, ZC, TYA_BOX, meta=meta,
        scratch=[vm((LV * 256, ZP)), vm((256, ZP)), vm((2 * KF * PG, MODES)), vm((KF, 128))], name="box")
    got_c, box_c = run(exchange_box_body, [((WD, 1, 128), F32), ((WD, 32, 128), BF)], spec_c, planes_c,
                       scratch=[DMA2, DMA2], cid=4, name="exchange_box")
    s_f, p_f, v_f = run(
        mix_f_body, [((4 * KF, 8 * CH), F32), ((WD, 2 * PF, 8 * CH), F32), ((8 * 2 * KF, CH), F32)],
        got_in, TXS_F, lift_f, got_c, TXS_BOX, fine_spectral[0], SPREAD_IN, FOLD_IN, TXB_F, meta=meta,
        scratch=[vm((GX, 2 * MODES)), vm((2 * FX, 8 * CH))], name="mix_f")
    (x_f,) = run(exchange_f_body, [((WD, 2 * PF, 8 * CH), F32)], p_f, scratch=[DMA2], cid=5, name="exchange_f")
    pred_f, send_f, pt_f = run(
        field_f_body, [((256, FZ), BF), ((KF, 2, 2 * PF, 8 * CH), F32), ((32, 128), BF)],
        x_f.reshape(KF, 2, 2 * PF, 8 * CH), PERM_IN, TYI_F, ZI_F, feat_f, lift_f, mixing_f, row_f, TILE_CL, SUM_CL,
        box_c, Z_UP, ROWS_UP, fine_cotangent[0], ONES_CL, ZF_F, TYF_F, PERM_OUT, ROWS_DOWN, Z_DOWN, meta=meta,
        scratch=[vm((128, MODES * CH), BF), vm((256, FZ)), vm((512, MODES * CH), BF), vm((256, ZP * CL)),
                 vm((256, ZP * CL)), vm((FY // 2, ZP))], name="field_f")
    got_f, pts = run(exchange_dual_body, [((WD, 2 * PF, 8 * CH), F32), ((WD, 32, 128), BF)],
                     send_f.reshape(WD, 2 * PF, 8 * CH), pt_f, scratch=[DMA2, DMA2], cid=6, name="exchange_dual")
    dual_f, q_f, mine = run(
        dual_f_body, [((4 * KF, 8 * CH), BF), ((WD, 1, 128), F32), ((128, 128), BF)],
        got_f, TXD_F, v_f, TXB_BOX, pts, meta=meta,
        scratch=[vm((2 * GX + 2 * GX, 8)), vm((2 * GX, 8))], name="dual_f")
    q_all, pt_all = run(exchange_back_body, [((LV, WD, 1, 128), F32), ((LV, 128, 128), BF)], q_f, mine,
                        scratch=[DMA2, DMA2, DMA2], cid=7, name="exchange_back")
    (send_g,) = run(
        back_g_body, [((LV, 64, MODES * CH), BF)],
        q_all, DD_BOX, TYB_BOX, pt_all, coarse_cotangent, slope_g, row_g, TILE_CL, ONES_CL, ZF_G, TYF_G, PERM_OUT,
        meta=meta, scratch=[vm((256, ZP)), vm((LV, PG, 224, 128)), vm((512, MODES * CH), BF)], name="back_g")
    (got_g,) = run(exchange_out_body, [((WD, 8, 128), F32)], send_g,
                   scratch=[vm((LV, 64, MODES * CH), BF), vm((8, 8, 8, 128)), DMA2, DMA2], cid=8, name="exchange_out")
    (grad_g,) = run(dual_g_body, [((2, KF, 2, CC), F32)], got_g, TXD_G, s_g, SPREAD_IN, SPREAD_OUT,
                    scratch=[vm((4 * KF, 2 * CH), BF)], name="dual_g")
    (grad_f,) = run(grad_f_body, [((8, KF, 2, CC), F32)], s_f, dual_f, SPREAD_IN, SPREAD_OUT, name="grad_f")
    coarse_out = pred_g.reshape(YG, PG, ZP).transpose(1, 0, 2)[:, :, :GZ].reshape(PG, YG * GZ)
    fine_out = pred_f.reshape(FY, PF, FZ).transpose(1, 0, 2).reshape(1, PF, FY * FZ)
    return coarse_out, fine_out, grad_g, grad_f[None]


def solution(mesh):
    placed = (
        P("wide", "level"),
        P("level", "wide", None),
        P("wide", "level"),
        P("level", "wide", None),
        P(),
        P(),
        P(),
        P(),
        P(("level", "wide"), None, None, None),
        P(),
        P("level", None, None),
        P("level", None, None),
        P("level", "wide", None, None, None),
        P("level", None),
    )
    return jax.shard_map(
        shards,
        mesh=mesh,
        in_specs=placed,
        out_specs=(
            P("wide", "level"),
            P("level", "wide", None),
            P(("level", "wide"), None, None, None),
            P("level", "wide", None, None, None),
        ),
        check_vma=False,
    )
```

time: 621 us -> 222 us (0.36); the launches traced: 610 us -> 222 us
  Pallas kernels: 0 us -> 198 us
  waiting for transfers between devices: 180 us -> 0 us
  matrix products: 131 us -> 0 us
  local copies, waits for them, and re-layouts: 109 us -> 21 us
  blocking collectives: 77.3 us -> 0 us
  starting transfers between devices: 68 us -> 0 us
  other arithmetic: 28.1 us -> 0.66 us
  between operations: 16.6 us -> 2.06 us
    pallas_call x0 -> x19, Pallas kernels: none -> 198 us  [run(): pl.pallas_call(body, out_shape=[jax.ShapeDtypeStruct(s, d) for s, d in ou...]
    all_to_all x9 -> x0, waiting for transfers between devices: 142 us -> none  [the longest x1 50.9 us: shards(): lax.all_to_all(lax.all_to_all(outgoing.astype(jnp.bfloat16), 'level', spl...]
    dot_general x64 -> x0, matrix products: 131 us -> none  [the longest x4 24.1 us: along_y(): return jnp.einsum('xypkc,ypqj->jkxqc', parts, table, precision=HIGH)]
    all_to_all x9 -> x0, starting transfers between devices: 67.9 us -> none  [the longest x4 33.8 us: to_modes(): lax.all_to_all(blocks, 'wide', split_axis=0, concat_axis=1, tiled=True)]
    all_to_all x2 -> x0, blocking collectives: 56.3 us -> none  [the longest x1 28.5 us: shards(): lax.all_to_all(outgoing.astype(jnp.bfloat16), 'level', split_axis=0, conc...]
    reduce_scatter x2 -> x0, waiting for transfers between devices: 38.6 us -> none  [coarse_forward(): lax.psum_scatter(along_y(spectra, cosine, sine_part), 'level', scatter_di...]
    another operation x10 -> x0, local copies, waits for them, and re-layouts: 32 us -> none  [the longest x2 17.4 us: shards(): fine_features = fine_input[0].reshape(fine_planes, FY, FZ, CIN)]
    reshape x13 -> x4, local copies, waits for them, and re-layouts: 24.8 us -> 2.98 us  [the longest x2 2.2 us: shards(): pred_f.reshape(FY, PF, FZ).transpose(1, 0, 2).reshape(1, PF, FY * FZ)]
  transfers between devices with their start and end apart: 11 -> 0, of which waited for: 11 -> 0; matrix products, arithmetic and copies ran while one was open for 12% -> 0% of each run, Pallas kernels for 0% -> 0%
where the time goes in v1:
time: 222 us
  Pallas kernels  198 us (89%)
  local copies, waits for them, and re-layouts  21 us (9%)
    pallas_call x19, Pallas kernels, run(): pl.pallas_call(body, out_shape=[jax.ShapeDtypeStruct(s, d) for s, d in ou...  198 us
    unnamed x118, local copies, waits for them, and re-layouts  14.7 us

profile of v1, /device:TPU:1, one launch (start us, length us, event | category | flops | bytes accessed | tf_op | source)
XLA Modules:
  0.0 221.7 jit_solution(17773436744843598320)
XLA Ops:
  0.7 1.3 dynamic_slice.7
  2.6 1.2 dynamic_slice.6
  9.3 1.6 copy-done.4
  12.6 1.5 features_g.1
  14.1 23.6 %exchange_in.1.u_ref = f32[64,8,128]{2,1,0:T(8,128)S(1)} custom-call(f32[32,4,128]{2,1,0:T(4,128)S(1)} %get-tuple-element.29.kg_ref, f32[32,2,128]{2,1,0:T(2,128)S(1)} %get-tuple-element.30.kf_ref), custom_call_target="tpu_custom_call" | custom-call | tf_op jit(solution)/shard_map/exchange_in/pallas_call | solution.py:186
  37.9 3.2 %mix_g.1 = (f32[128,96]{1,0:T(8,128)S(1)}, f32[64,8,128]{2,1,0:T(8,128)S(1)}) custom-call(s32[8]{0:T(128)S(1)} %concatenate.3.meta, f32[64,8,128]{2,1,0:T(8,128)S(1)} %exchange_in.1.u_ref, f32[128,1024]{1,0:T(8,128)S(1)} %copy-done.16, bf16[4,48]{1,0:T(4,128)(2,1)S(1)} %copy-done.56, bf16[2,32,2,2304]{3,2,1,0:T(2,128)(2,1)S(1)} %copy-done.13, ...), custom_call_target="tpu_custom_call" | custom-call | tf_op jit(solution)/shard_map/mix_g/pallas_call | solution.py:186
  41.1 22.0 %exchange_g.1.x_ref = bf16[4,512,128]{2,1,0:T(8,128)(2,1)S(1)} custom-call(f32[64,8,128]{2,1,0:T(8,128)S(1)} %get-tuple-element.31.p_ref), custom_call_target="tpu_custom_call" | custom-call | tf_op jit(solution)/shard_map/exchange_g/pallas_call | solution.py:186
  63.2 4.8 %field_g.1 = (bf16[256,64]{1,0:T(8,128)(2,1)S(1)}, bf16[6,256,512]{2,1,0:T(8,128)(2,1)S(1)}) custom-call(s32[8]{0:T(128)S(1)} %concatenate.3.meta, bf16[4,512,128]{2,1,0:T(8,128)(2,1)S(1)} %exchange_g.1.x_ref, bf16[1024,768]{1,0:T(8,128)(2,1)S(1)} %copy-done.7, bf16[4,512,256]{2,1,0:T(8,128)(2,1)S(1)} %copy-done.10, bf16[256,512]{1,0:T(8,128)(2,1)S(1)} %copy-done.23, ...), custom_call_target="tpu_custom_call" | custom-call | tf_op jit(solution)/shard_map/field_g/pallas_call | solution.py:186
  69.9 5.8 %gather_rows.1.rows_ref = bf16[4,256,64]{2,1,0:T(8,128)(2,1)S(1)} custom-call(bf16[256,64]{1,0:T(8,128)(2,1)S(1)} %get-tuple-element.33.x_ref), custom_call_target="tpu_custom_call" | custom-call | tf_op jit(solution)/shard_map/gather_rows/pallas_call | solution.py:186
  75.8 1.6 box.1
  77.4 22.3 %exchange_box.1 = (f32[64,1,128]{2,1,0:T(1,128)S(1)}, bf16[64,32,128]{2,1,0:T(8,128)(2,1)S(1)}) custom-call(f32[32,1,128]{2,1,0:T(1,128)S(1)} %get-tuple-element.34.spec_ref, bf16[4,32,128]{2,1,0:T(8,128)(2,1)S(1)} %get-tuple-element.35.planes_ref), custom_call_target="tpu_custom_call" | custom-call | tf_op jit(solution)/shard_map/exchange_box/pallas_call | solution.py:186
  99.8 1.7 copy-done.3
  101.6 8.7 %mix_f.1 = (f32[128,384]{1,0:T(8,128)S(1)}, f32[64,4,384]{2,1,0:T(4,128)S(1)}, f32[512,48]{1,0:T(8,128)S(1)}) custom-call(s32[8]{0:T(128)S(1)} %concatenate.3.meta, f32[64,8,128]{2,1,0:T(8,128)S(1)} %exchange_in.1.u_ref, f32[128,1024]{1,0:T(8,128)S(1)} %copy-done.17, bf16[5,48]{1,0:T(8,128)(2,1)S(1)} %bitcast.28, f32[64,1,128]{2,1,0:T(1,128)S(1)} %get-tuple-element.36.c_ref, ...), custom_call_target="tpu_custom_call" | custom-call | tf_op jit(solution)/shard_map/mix_f/pallas_call | solution.py:186
  110.3 17.9 %exchange_f.1 = f32[64,4,384]{2,1,0:T(4,128)S(1)} custom-call(f32[64,4,384]{2,1,0:T(4,128)S(1)} %get-tuple-element.37.x_ref), custom_call_target="tpu_custom_call" | custom-call | tf_op jit(solution)/shard_map/exchange_f/pallas_call | solution.py:186
  128.4 8.6 %field_f.1 = (bf16[256,64]{1,0:T(8,128)(2,1)S(1)}, f32[32,2,4,384]{3,2,1,0:T(4,128)S(1)}, bf16[32,128]{1,0:T(8,128)(2,1)S(1)}) custom-call(s32[8]{0:T(128)S(1)} %concatenate.3.meta, f32[32,2,4,384]{3,2,1,0:T(4,128)S(1)} %bitcast.21, bf16[768,768]{1,0:T(8,128)(2,1)S(1)} %copy-done.8, bf16[512,128]{1,0:T(8,128)(2,1)S(1)} %copy-done.35, ...), custom_call_target="tpu_custom_call" | custom-call | tf_op jit(solution)/shard_map/field_f/pallas_call | solution.py:186
  137.6 1.6 reshape.33
  139.2 28.2 %exchange_dual.1 = (f32[64,4,384]{2,1,0:T(4,128)S(1)}, bf16[64,32,128]{2,1,0:T(8,128)(2,1)S(1)}) custom-call(f32[64,4,384]{2,1,0:T(4,128)S(1)} %bitcast.22, bf16[32,128]{1,0:T(8,128)(2,1)S(1)} %get-tuple-element.42.pt_ref), custom_call_target="tpu_custom_call" | custom-call | tf_op jit(solution)/shard_map/exchange_dual/pallas_call | solution.py:186
  169.3 1.9 dual_f.1
  171.2 15.4 %exchange_back.1 = (f32[4,64,1,128]{3,2,1,0:T(1,128)S(1)}, bf16[4,128,128]{2,1,0:T(8,128)(2,1)S(1)}) custom-call(f32[64,1,128]{2,1,0:T(1,128)S(1)} %get-tuple-element.46.q_ref, bf16[128,128]{1,0:T(8,128)(2,1)S(1)} %get-tuple-element.47.pt_ref), custom_call_target="tpu_custom_call" | custom-call | tf_op jit(solution)/shard_map/exchange_back/pallas_call | solution.py:186
  186.6 1.2 copy-done.9
  189.8 3.4 %back_g.1.x_ref = bf16[4,64,768]{2,1,0:T(8,128)(2,1)S(1)} custom-call(s32[8]{0:T(128)S(1)} %concatenate.3.meta, f32[4,64,1,128]{3,2,1,0:T(1,128)S(1)} %get-tuple-element.48.q_ref, bf16[128,1024]{1,0:T(8,128)(2,1)S(1)} %copy-done.20, f32[4,448,64]{2,1,0:T(8,128)S(1)} %copy-done.11, bf16[4,128,128]{2,1,0:T(8,128)(2,1)S(1)} %get-tuple-element.49.pt_ref, ...), custom_call_target="tpu_custom_call" | custom-call | tf_op jit(solution)/shard_map/back_g/pallas_call | solution.py:186
  193.3 21.6 %exchange_out.1.z_ref = f32[64,8,128]{2,1,0:T(8,128)S(1)} custom-call(bf16[4,64,768]{2,1,0:T(8,128)(2,1)S(1)} %back_g.1.x_ref), custom_call_target="tpu_custom_call" | custom-call | tf_op jit(solution)/shard_map/exchange_out/pallas_call | solution.py:186
  214.9 1.9 dual_g.1
  216.8 5.0 %grad_f.1 = f32[8,32,2,2304]{3,2,1,0:T(2,128)} custom-call(f32[128,384]{1,0:T(8,128)S(1)} %copy-done.28, bf16[128,384]{1,0:T(8,128)(2,1)S(1)} %get-tuple-element.53.d_ref, bf16[48,2304]{1,0:T(8,128)(2,1)S(1)} %copy-done.1, bf16[48,2304]{1,0:T(8,128)(2,1)S(1)} %copy-done.12), custom_call_target="tpu_custom_call" | custom-call | tf_op jit(solution)/shard_map/grad_f/pallas_call | solution.py:186
  (121 shorter events, 13.8 us)
Async XLA Ops:
  0.6 37.1 %copy-start.1 = (bf16[48,2304]{1,0:T(8,128)(2,1)S(1)}, bf16[48,2304]{1,0:T(8,128)(2,1)}, u32[]{:S(2)}) copy-start(bf16[48,2304]{1,0:T(8,128)(2,1)} %constant.97.clone.e_ref) | copy-start | bytes 663556
  0.6 37.1 %copy-start.2 = (bf16[2304,48]{1,0:T(8,128)(2,1)S(1)}, bf16[2304,48]{1,0:T(8,128)(2,1)}, u32[]{:S(2)}) copy-start(bf16[2304,48]{1,0:T(8,128)(2,1)} %constant.98.clone.r_ref) | copy-start | bytes 663556
  41.1 26.9 %copy-start.45 = (f32[128,96]{1,0:T(8,128)}, f32[128,96]{1,0:T(8,128)S(1)}, u32[]{:S(2)}) copy-start(f32[128,96]{1,0:T(8,128)S(1)} %get-tuple-element.51.s_ref) | copy-start | bytes 147460
  63.2 36.6 %copy-start.42 = (bf16[256,128]{1,0:T(8,128)(2,1)S(1)}, bf16[256,128]{1,0:T(8,128)(2,1)}, u32[]{:S(2)}) copy-start(bf16[256,128]{1,0:T(8,128)(2,1)} %constant.109.clone.tb_ref) | copy-start | bytes 196612
  63.2 36.6 %copy-start.43 = (f32[128,128]{1,0:T(8,128)S(1)}, f32[128,128]{1,0:T(8,128)}, u32[]{:S(2)}) copy-start(f32[128,128]{1,0:T(8,128)} %constant.108.clone.txc_ref) | copy-start | bytes 196612
  63.2 36.6 %copy-start.55 = (bf16[1,5,48]{2,1,0:T(8,128)(2,1)S(1)}, bf16[1,5,48]{2,1,0:T(8,128)(2,1)}, u32[]{:S(2)}) copy-start(bf16[1,5,48]{2,1,0:T(8,128)(2,1)} %param.61) | copy-start | bytes 1444
  69.2 30.6 %copy-start.17 = (f32[128,1024]{1,0:T(8,128)S(1)}, f32[128,1024]{1,0:T(8,128)}, u32[]{:S(2)}) copy-start(f32[128,1024]{1,0:T(8,128)} %constant.107.clone.tx_ref) | copy-start | bytes 1572868
  101.4 26.8 %copy-start.8 = (bf16[768,768]{1,0:T(8,128)(2,1)S(1)}, bf16[768,768]{1,0:T(8,128)(2,1)}, u32[]{:S(2)}) copy-start(bf16[768,768]{1,0:T(8,128)(2,1)} %constant.110.clone.perm_ref) | copy-start | bytes 3538948
  101.5 26.8 %copy-start.18 = (bf16[64,512]{1,0:T(8,128)(2,1)S(1)}, bf16[64,512]{1,0:T(8,128)(2,1)}, u32[]{:S(2)}) copy-start(bf16[64,512]{1,0:T(8,128)(2,1)} %constant.115.clone.ones_ref) | copy-start | bytes 196612
  101.5 26.8 %copy-start.21 = (bf16[512,256]{1,0:T(8,128)(2,1)S(1)}, bf16[512,256]{1,0:T(8,128)(2,1)}, u32[]{:S(2)}) copy-start(bf16[512,256]{1,0:T(8,128)(2,1)} %constant.116.clone.zf_ref) | copy-start | bytes 786436
  101.5 26.8 %copy-start.22 = (bf16[256,512]{1,0:T(8,128)(2,1)S(1)}, bf16[256,512]{1,0:T(8,128)(2,1)}, u32[]{:S(2)}) copy-start(bf16[256,512]{1,0:T(8,128)(2,1)} %constant.112.clone.zi_ref) | copy-start | bytes 786436
  101.5 26.8 %copy-start.33 = (bf16[128,512]{1,0:T(8,128)(2,1)S(1)}, bf16[128,512]{1,0:T(8,128)(2,1)}, u32[]{:S(2)}) copy-start(bf16[128,512]{1,0:T(8,128)(2,1)} %constant.117.clone.tyf_ref) | copy-start | bytes 393220
  101.5 26.8 %copy-start.34 = (bf16[2,256,32]{2,1,0:T(8,128)(2,1)S(1)}, bf16[2,256,32]{2,1,0:T(8,128)(2,1)}, u32[]{:S(2)}) copy-start(bf16[2,256,32]{2,1,0:T(8,128)(2,1)} %constant.114.clone.rup_ref) | copy-start | bytes 98308
  101.5 26.8 %copy-start.35 = (bf16[512,128]{1,0:T(8,128)(2,1)S(1)}, bf16[512,128]{1,0:T(8,128)(2,1)}, u32[]{:S(2)}) copy-start(bf16[512,128]{1,0:T(8,128)(2,1)} %constant.111.clone.ty_ref) | copy-start | bytes 393220
  101.5 26.8 %copy-start.38 = (bf16[256,256]{1,0:T(8,128)(2,1)S(1)}, bf16[256,256]{1,0:T(8,128)(2,1)}, u32[]{:S(2)}) copy-start(bf16[256,256]{1,0:T(8,128)(2,1)} %copy-done.37) | copy-start | bytes 393220
  101.5 26.8 %copy-start.40 = (f32[1,2,8192]{2,1,0:T(2,128)S(1)}, f32[1,2,8192]{2,1,0:T(2,128)}, u32[]{:S(2)}) copy-start(f32[1,2,8192]{2,1,0:T(2,128)} %param.54) | copy-start | bytes 196612
  101.5 26.8 %copy-start.41 = (f32[64,256]{1,0:T(8,128)S(1)}, f32[64,256]{1,0:T(8,128)}, u32[]{:S(2)}) copy-start(f32[64,256]{1,0:T(8,128)} %constant.119.clone.rdn_ref) | copy-start | bytes 196612
  101.5 26.8 %copy-start.50 = (f32[64,64]{1,0:T(8,128)S(1)}, f32[64,64]{1,0:T(8,128)}, u32[]{:S(2)}) copy-start(f32[64,64]{1,0:T(8,128)} %constant.120.clone.zdn_ref) | copy-start | bytes 49156
  101.6 26.8 %copy-start.52 = (bf16[64,64]{1,0:T(8,128)(2,1)S(1)}, bf16[64,64]{1,0:T(8,128)(2,1)}, u32[]{:S(2)}) copy-start(bf16[64,64]{1,0:T(8,128)(2,1)} %constant.113.clone.zup_ref) | copy-start | bytes 24580
  101.6 26.8 %copy-start.54 = (bf16[1,48,48]{2,1,0:T(8,128)(2,1)S(1)}, bf16[1,48,48]{2,1,0:T(8,128)(2,1)}, u32[]{:S(2)}) copy-start(bf16[1,48,48]{2,1,0:T(8,128)(2,1)} %param.62) | copy-start | bytes 13828
  128.4 39.1 %copy-start.44 = (f32[128,128]{1,0:T(8,128)S(1)}, f32[128,128]{1,0:T(8,128)}, u32[]{:S(2)}) copy-start(f32[128,128]{1,0:T(8,128)} %constant.122.clone.tb_ref) | copy-start | bytes 196612
  137.0 49.6 %copy-start.6 = (bf16[6,256,512]{2,1,0:T(8,128)(2,1)S(1)}, bf16[6,256,512]{2,1,0:T(8,128)(2,1)}, u32[]{:S(2)}) copy-start(bf16[6,256,512]{2,1,0:T(8,128)(2,1)} %copy-done.5) | copy-start | bytes 4718596
  139.2 47.4 %copy-start.19 = (bf16[512,256]{1,0:T(8,128)(2,1)S(1)}, bf16[512,256]{1,0:T(8,128)(2,1)}, u32[]{:S(2)}) copy-start(bf16[512,256]{1,0:T(8,128)(2,1)} %constant.125.clone.zf_ref) | copy-start | bytes 786436
  139.2 47.4 %copy-start.20 = (bf16[128,1024]{1,0:T(8,128)(2,1)S(1)}, bf16[128,1024]{1,0:T(8,128)(2,1)}, u32[]{:S(2)}) copy-start(bf16[128,1024]{1,0:T(8,128)(2,1)} %constant.123.clone.dd_ref) | copy-start | bytes 786436
  (35 other events, 514.3 us)

commit v2 on v1

v2 whole, which is shorter than its diff:
```python
import math

import ml_dtypes
import numpy as np
import jax
import jax.numpy as jnp
from jax import lax
from jax.experimental import pallas as pl
from jax.experimental.pallas import tpu as pltpu
from jax.sharding import PartitionSpec as P

MODES = 16
KF = 2 * MODES
CH = 48
NB = 6
CL = 8
GX = 256
GY = 256
GZ = 50
FX = 128
FY = 128
FZ = 64
ZP = 64
LV = 4
WD = 64
PG = 4
YG = 64
PF = 2
CC = CH * CH
BF = jnp.bfloat16
F32 = jnp.float32
HIGH = lax.Precision.HIGHEST
VMEM_BYTES = 60 * 2**20


def bf(x):
    return np.asarray(x, np.float32).astype(ml_dtypes.bfloat16)


def f32(x):
    return np.asarray(x, np.float32)


def waves(rows, length):
    j = np.arange(KF)
    signed = np.where(j < MODES, j, j - KF)
    turn = np.mod(rows[:, None] * signed[None, :], length) * (2.0 * math.pi / length)
    return np.cos(turn) / math.sqrt(length), np.sin(turn) / math.sqrt(length)


def forward_table(rows, length):
    c, s = waves(rows, length)
    c, s = c.T, s.T
    return np.stack([np.stack([c, s], 1), np.stack([-s, c], 1)], 0)


def depth(length):
    c, s = waves(np.arange(length), length)
    both = np.stack([c[:, :MODES], -s[:, :MODES]], 1)
    both = bf(both).astype(np.float64)
    return np.concatenate([both, np.zeros((ZP - length, 2, MODES))], 0)


D_G, D_F = depth(GZ), depth(FZ)
ZMAP = np.zeros((ZP, FZ))
ZMAP[np.arange(FZ) * GZ // FZ, np.arange(FZ)] = 1.0
D_POOL = np.einsum("gf,frk->grk", ZMAP, D_F)


def depth_blocks(d):
    return np.einsum("zrk,ij->zirkj", d, np.eye(CL)).reshape(ZP * CL, 2 * MODES * CL)


def depth_features(d, length):
    return np.einsum("zrk,ij->zirkj", d[:length], np.eye(4)).reshape(length * 4, 2 * MODES * 4)


ZF_G, ZF_F = bf(depth_blocks(D_G)), bf(depth_blocks(D_F))
ZI_G, ZI_F = bf(depth_blocks(D_G).T), bf(depth_blocks(D_F).T)
Z4_G, Z4_F = bf(depth_features(D_G, GZ)), bf(depth_features(D_F, FZ))
ZC = f32(D_POOL.reshape(ZP, 2 * MODES))

FY_G = np.stack([forward_table(v * YG + np.arange(YG), GY) for v in range(LV)], 0)
FY_F = forward_table(np.arange(FY), FY)
FY_BOX = FY_F.reshape(2, KF, 2, FY // 2, 2).sum(4)
FX_G = forward_table(np.arange(GX), GX)
FX_F = forward_table(np.arange(FX), FX)
FX_BOX = FX_F.reshape(2, KF, 2, FX // 2, 2).sum(4)
EYE_G, EYE_F = np.eye(PG), np.eye(PF)

TYA_G = f32(np.einsum("vakbt,pq->vakpbtq", FY_G, EYE_G).reshape(LV, 2 * KF * PG, 2 * YG * PG))
TYA_F = f32(np.einsum("akbt,pq->akpbtq", FY_F, EYE_F).reshape(2 * KF * PF, 2 * FY * PF))
TYA_BOX = f32(np.einsum("akbt,pq->akpbtq", FY_BOX, EYE_G).reshape(2 * KF * PG, FY * PG))
TYF_G = bf(np.einsum("vakbt,pq->vkpabtq", FY_G, EYE_G).reshape(LV, KF * PG * 2, 2 * YG * PG))
TYF_F = bf(np.einsum("akbt,pq->kpabtq", FY_F, EYE_F).reshape(KF * PF * 2, 2 * FY * PF))
TYI_G = bf(np.einsum("vbkat,pq->vatpkqb", FY_G, EYE_G).reshape(LV, 2 * YG * PG, KF * PG * 2))
TYI_F = bf(np.einsum("bkat,pq->atpkqb", FY_F, EYE_F).reshape(2 * FY * PF, KF * PF * 2))
TYB_BOX = bf(np.repeat(FY_BOX.transpose(3, 2, 0, 1).reshape(FY // 2, 4 * KF), 2, axis=1))
DD_BOX = bf(np.einsum("zahk,pq,rs->hprkasqz", D_POOL.reshape(ZP, 2, 2, 8), EYE_G, np.eye(2)).reshape(128, 4 * PG * ZP))


def source_rows(table):
    a = np.stack([table[0], -table[1]], 1)
    b = np.stack([table[1], table[0]], 1)
    return np.stack([a, b], 0).reshape(4 * KF, 2, -1)


def in_rows(table, planes, first):
    rows = source_rows(table).reshape(4 * KF, 2, WD, planes)
    out = np.zeros((4 * KF, 2, WD, 8))
    out[..., first : first + planes] = rows
    return out.reshape(4 * KF, 2 * WD * 8)


TXS_G = f32(in_rows(FX_G, PG, 0))
TXS_F = f32(in_rows(FX_F, PF, PG))
TXS_BOX = f32(source_rows(FX_BOX).reshape(4 * KF, FX))


def dual_rows(table, count):
    r, i = table[0], table[1]
    kinds = [np.stack([r, r], 1), np.stack([i, i], 1), np.stack([r, i], 1), np.stack([i, -r], 1)]
    rows = np.stack(kinds[:count], 0).transpose(0, 1, 2, 4, 3)
    return rows.reshape(count * 2 * KF, -1)


TXD_G = bf(dual_rows(FX_G, 2))
TXD_F = bf(dual_rows(FX_F, 4))


def back_rows(table):
    back = table.transpose(3, 2, 0, 1)
    back = np.stack([back, back], 4)
    return back.reshape(back.shape[0] * 2, 4 * KF)


TXB_G = bf(back_rows(FX_G))
TXB_F = bf(back_rows(FX_F))
TXB_BOX = f32(back_rows(FX_BOX))

PERM = np.zeros((MODES, NB, CL, NB, MODES, CL))
for _k in range(MODES):
    for _b in range(NB):
        for _l in range(CL):
            PERM[_k, _b, _l, _b, _k, _l] = 1.0
PERM = PERM.reshape(MODES * CH, MODES * CH)
PERM_OUT = bf(PERM.T)
PERM_WIDE = np.zeros((8, 128, MODES * CH))
PERM_WIDE[:, : 2 * CH] = PERM.reshape(8, 2 * CH, MODES * CH)
PERM_WIDE = PERM_WIDE.reshape(1024, MODES * CH)
PERM_WIDE, PERM_WIDE_OUT = bf(PERM_WIDE), bf(PERM_WIDE.T)
SPREAD_IN = bf(np.kron(np.eye(CH), np.ones((1, CH))))
CHUNK = 8 * CH
TILE_OUT = bf(np.kron(np.ones((1, 8)), np.eye(CH)))
FOLD = bf(np.kron(np.ones((8, 1)), np.eye(CH)))
ONES_CL = bf(np.kron(np.eye(ZP), np.ones((1, CL))))
SUM_CL = bf(np.kron(np.eye(ZP), np.ones((CL, 1))))
TILE_CL = f32(np.kron(np.ones((1, ZP)), np.eye(CL)))
ROWS_UP = np.kron(np.eye(FY // 2), np.ones((2 * PF, 1))).reshape(256, FY // 4, 2).transpose(2, 0, 1)
ROWS_UP = bf(ROWS_UP)
ROWS_DOWN = f32(np.kron(np.eye(FY // 2), np.ones((1, 2 * PF))))
Z_UP = bf(ZMAP)
Z_DOWN = f32(ZMAP.T)


def mm(a, b):
    return jnp.dot(a, b, preferred_element_type=F32)


def mmh(a, b):
    return jnp.dot(a, b, preferred_element_type=F32, precision=HIGH)


MESH = pl.DeviceIdType.MESH
DMA2 = pltpu.SemaphoreType.DMA((2,))


def vm(shape, kind=F32):
    return pltpu.VMEM(shape, kind)


BY_LEVEL = ("tya_g", "tyi_g", "tyf_g")


def run(body, outs, smem, inputs, scratch, sems=(), kept=(), cid=None, name=None):
    held = {n: vm(t.shape[1:] if n in BY_LEVEL else t.shape, t.dtype) for n, t in inputs.items()}

    def kernel(*refs):
        refs = list(refs)

        def take(names):
            got = {n: refs.pop(0) for n in names}
            return got

        scalars = take(smem)
        given = take(inputs)
        res = take(outs)
        scr = take(scratch)
        sem = take(sems)
        inside = take(held)
        load_sem = refs.pop(0)
        level = lax.axis_index("level")
        copies, started, ready = {}, set(), set()
        for k, n in enumerate(inputs):
            src = given[n].at[level] if n in BY_LEVEL else given[n]
            copies[n] = pltpu.make_async_copy(src, inside[n], load_sem.at[k])

        def start(names):
            for n in names:
                if n not in started:
                    copies[n].start()
                    started.add(n)

        def get(n):
            if n not in ready:
                copies[n].wait()
                ready.add(n)
            return inside[n]

        body(scalars, start, get, res, scr, sem)

    got = pl.pallas_call(
        kernel,
        out_shape=[jax.ShapeDtypeStruct(s, d) for s, d in outs.values()],
        in_specs=[pl.BlockSpec(memory_space=pltpu.SMEM)] * len(smem) + [pl.BlockSpec(memory_space=pl.ANY)] * len(inputs),
        out_specs=[pl.BlockSpec(memory_space=pl.ANY if n in kept else pltpu.VMEM) for n in outs],
        scratch_shapes=[vm(*v) for v in scratch.values()] + [DMA2] * len(sems) + list(held.values())
        + [pltpu.SemaphoreType.DMA((len(held),))],
        name=name,
        compiler_params=pltpu.CompilerParams(
            vmem_limit_bytes=VMEM_BYTES, collective_id=cid, has_side_effects=cid is not None),
    )(*smem.values(), *inputs.values())
    return dict(zip(outs, got))


def halves(u):
    half = u.shape[1] // 2
    return jnp.concatenate([u[:, :half], u[:, half:]], axis=0)


def features(rows, planes, width, x_ref, z, table, feat_ref, out_ref, scr):
    for y in range(rows):
        scr[planes * y : planes * (y + 1), :] = x_ref[:, width * y : width * (y + 1)].astype(F32)
    feat = scr[...].astype(BF)
    feat_ref[...] = feat
    both = mmh(table, halves(mm(feat, z)))
    rows_out = both.shape[0] // 2
    lanes = jnp.concatenate([both[:rows_out], both[rows_out:]], axis=1)
    out_ref[...] = lanes.reshape(out_ref.shape)


def stack_modes(x, modes, lane):
    return jnp.concatenate([x[:, lane(m) : lane(m) + CH] for m in range(modes)], axis=0).astype(BF)


def lane_g(m):
    return CH * m


def lane_f(m):
    return 128 * (m // 2) + CH * (m % 2)


def weights_chunk(w_ref, c):
    w = w_ref[:, :, :, CHUNK * c : CHUNK * (c + 1)].astype(F32)
    return w.reshape(w.shape[0] * 2 * KF, CHUNK)


def mix_modes(s, modes, w_ref, spread, fold, table, acc_a, acc_b):
    half = 2 * KF
    sa, sb = stack_modes(s[:half], modes, lane_g), stack_modes(s[half:], modes, lane_g)
    for c in range(CC // CHUNK):
        w = weights_chunk(w_ref, c)
        e = spread[:, CHUNK * c : CHUNK * (c + 1)]
        if c == 0:
            acc_a[...] = w * mm(sa, e)
            acc_b[...] = w * mm(sb, e)
        else:
            acc_a[...] += w * mm(sa, e)
            acc_b[...] += w * mm(sb, e)
    pa, pb = mm(acc_a[...].astype(BF), fold).astype(BF), mm(acc_b[...].astype(BF), fold).astype(BF)
    spare = jnp.zeros((2 * half, 128 - 2 * CH), BF)
    parts = []
    for m in range(modes):
        parts.append(jnp.concatenate([pa[half * m : half * (m + 1)], pb[half * m : half * (m + 1)]], axis=0))
        if m % 2 == 1:
            parts.append(spare)
    return mm(table, jnp.concatenate(parts, axis=1))


def grad_modes(sa, sb, za, zb, spread, put):
    for c in range(CC // CHUNK):
        e = spread[:, CHUNK * c : CHUNK * (c + 1)]
        g = mm(sa, e) * za + mm(sb, e) * zb
        put(slice(CHUNK * c, CHUNK * (c + 1)), g.reshape(g.shape[0] // (2 * KF), KF, 2, CHUNK))


def shift_rows(rows, cols, by, group_rows=None):
    r = lax.broadcasted_iota(jnp.int32, (rows, cols), 0)
    c = lax.broadcasted_iota(jnp.int32, (rows, cols), 1)
    hit = c - r == by
    if group_rows is not None:
        shift = group_rows.bit_length() - 1
        hit = jnp.logical_and(hit, lax.shift_right_logical(r, shift) == lax.shift_right_logical(c, shift))
    return jnp.where(hit, 1.0, 0.0)


def pick_plane(planes, at):
    which = lax.broadcasted_iota(jnp.int32, planes.shape, 0)
    return jnp.sum(jnp.where(which == at, planes, 0.0), axis=0)


def pair_rows(scr, first, stride, count):
    even = scr[pl.ds(first, count, stride=2 * stride), :]
    odd = scr[pl.ds(first + stride, count, stride=2 * stride), :]
    return jnp.concatenate([even, odd], axis=1)


def selector(lift, count, first, features_in):
    shape = (MODES * features_in, count * CH)
    rows = lax.broadcasted_iota(jnp.int32, shape, 0)
    cols = lax.broadcasted_iota(jnp.int32, shape, 1)
    tiled = jnp.concatenate([lift] * MODES, axis=0) if features_in > 1 else lift
    tiled = jnp.concatenate([tiled] * count, axis=1)
    mode = sum((cols >= CH * m).astype(jnp.int32) for m in range(1, count))
    kz = lax.shift_right_logical(rows, 2) if features_in > 1 else rows
    return jnp.where(kz == first + mode, tiled, 0.0)


K0 = math.sqrt(2.0 / math.pi)


def gelu_parts(x):
    x2 = x * x
    t = jnp.tanh(K0 * x * (1.0 + 0.044715 * x2))
    hidden = 0.5 * x * (1.0 + t)
    slope = 0.5 * (1.0 + t) + 0.5 * x * (1.0 - t * t) * (K0 * (1.0 + 3.0 * 0.044715 * x2))
    return hidden, slope


def block_pre(bb, b, zi):
    rows = bb.shape[0] // 2
    lanes = slice(MODES * CL * b, MODES * CL * (b + 1))
    return mm(bb[:rows, lanes], zi[: MODES * CL]) + mm(bb[rows:, lanes], zi[MODES * CL :])


def lanes_of(row, b, tile):
    return mmh(row[:, CL * b : CL * (b + 1)], tile)


def point_block(point, b, tile, shift):
    count = point.shape[0]
    full = jnp.concatenate([lanes_of(point, b, tile)] * ZP, axis=0)
    z_row = lax.shift_right_logical(lax.broadcasted_iota(jnp.int32, full.shape, 0), shift)
    z_col = lax.shift_right_logical(lax.broadcasted_iota(jnp.int32, full.shape, 1), 3)
    return jnp.where(z_row == z_col, full, 0.0).astype(BF)


def split(x):
    top = x.astype(BF)
    return top, (x - top.astype(F32)).astype(BF)


def mm_split(x, table):
    top, low = split(x)
    return mm(top, table) + mm(low, table)


def put_block(a_scr, gp, b, zf):
    a = mm(gp, zf).astype(BF)
    rows = a.shape[0]
    width = MODES * CL
    a_scr[:rows, width * b : width * (b + 1)] = a[:, :width]
    a_scr[rows:, width * b : width * (b + 1)] = a[:, width:]


def forward_tail(a_scr, table, perm):
    return mm(mm(table, a_scr[...]).astype(BF), perm)


def here():
    return lax.axis_index("level"), lax.axis_index("wide")


def greet():
    level, wide = here()
    barrier = pltpu.get_barrier_semaphore()
    for i in range(1, LV):
        pl.semaphore_signal(barrier, inc=1, device_id=(lax.rem(level + i, LV), wide), device_id_type=MESH)

    def one(i, carry):
        pl.semaphore_signal(barrier, inc=1, device_id=(level, lax.rem(wide + i, WD)), device_id_type=MESH)
        return carry

    lax.fori_loop(1, WD, one, 0)
    return barrier, LV - 1 + WD - 1


def remote(src, dst, sems, to):
    return pltpu.make_async_remote_copy(
        src_ref=src, dst_ref=dst, send_sem=sems.at[0], recv_sem=sems.at[1], device_id=to, device_id_type=MESH)


def push_wide(source, land, sems):
    level, wide = here()

    def one(i, carry):
        peer = lax.rem(wide + i, WD)
        remote(source(peer), land.at[wide], sems, (level, peer)).start()
        return carry

    lax.fori_loop(1, WD, one, 0)


def push_level(source, land, sems):
    level, wide = here()
    for i in range(1, LV):
        peer = lax.rem(level + i, LV)
        remote(source(peer), land.at[level], sems, (peer, wide)).start()


def finish(land, sems, count):
    level, wide = here()
    part = land.at[pl.ds(0, count - 1)]
    done = remote(part, part, sems, (level, wide))
    done.wait_send()
    done.wait_recv()


SEMS = ("in_level", "in", "g", "g_level", "rows", "spec", "box", "f", "dual", "pts", "q", "q_level", "pt_level",
        "out_level", "got_g")
RESULTS = {
    "pred_g": ((256, ZP), F32), "pred_f": ((256, FZ), F32), "s_g": ((4 * KF, 2 * CH), F32),
    "s_f": ((4 * KF, 8 * CH), F32), "dual_f": ((4 * KF, 512), BF), "got_g": ((WD, 8, 128), F32),
}
LANDS = {
    "in_level": ((LV, 8, PG, 128), F32), "in": ((WD, 8, 128), F32), "g": ((WD, 8, 128), F32),
    "g_level": ((LV, WD * 8, 128), BF), "rows": ((LV, 256, ZP), BF), "spec": ((WD, 1, 128), F32),
    "box": ((WD, 32, 128), BF), "f": ((WD, 16, 128), BF), "dual": ((WD, 16, 128), BF), "pts": ((WD, 32, 128), BF),
    "q": ((LV, WD, 1, 128), F32), "pt_level": ((LV, 128, 128), BF), "out_level": ((LV, 64, MODES * CH), BF),
}
SCRATCH = {
    "x_g": ((256, GZ * 4), F32), "x_ff": ((256, FZ * 4), F32), "feat_g": ((256, GZ * 4), BF), "feat_f": ((256, FZ * 4), BF),
    "kg": ((KF, PG, 128), F32), "kf": ((KF, PF, 128), F32), "cot_f": ((256, FZ), F32),
    "msg_in": ((WD, 8, 128), F32), "p_gm": ((WD, 8, 128), F32), "mix_a": ((512, CHUNK), F32), "mix_b": ((512, CHUNK), F32),
    "mix_ga": ((128, CHUNK), F32), "mix_gb": ((128, CHUNK), F32), "wide_cot": ((256, ZP * CL), F32),
    "x_wide": ((KF, 8, 8, 128), F32), "x_in": ((256, 1024), BF), "acc": ((256, ZP * CL), F32),
    "acc_pt": ((256, ZP * CL), F32), "slope": ((NB, 256, ZP * CL), BF), "pred_b": ((256, ZP), BF),
    "box_f": ((256, ZP), F32), "s_box": ((2 * KF * PG, MODES), F32),
    "o_box": ((KF, 128), F32), "spec_m": ((KF, 1, 128), F32), "planes_m": ((PG, 32, 128), BF),
    "x_box": ((GX, 2 * MODES), F32), "p_f": ((4 * 2 * FX, 128), F32), "p_fm": ((WD, 16, 128), BF),
    "v_f": ((8 * 2 * KF, CH), F32), "lm_g": ((NB, GZ * 4, ZP * CL), BF), "lm_f": ((NB, FZ * 4, ZP * CL), BF),
    "lc_f": ((NB, FZ, ZP * CL), BF), "x_f": ((KF, 32, 128), F32), "x_fb": ((128, 1024), BF),
    "a": ((512, MODES * CH), BF), "m_f": ((KF, 32, 128), F32), "m_fm": ((WD, 16, 128), BF),
    "pt": ((FY // 2, ZP), F32), "pt_m": ((32, 128), BF), "d_f": ((4 * 2 * FX, 128), F32),
    "d_lanes": ((2 * FX, 512), BF), "q_rows": ((2 * GX, 8), F32),
    "q_m": ((WD, 1, 128), F32), "mine": ((128, 128), BF), "cot": ((256, ZP), F32),
    "send_g": ((LV, 64, MODES * CH), BF), "msg_out": ((8, 8, 8, 128), F32),
}
FIRST = ("x_in_f", "z4_f", "tya_f", "x_in_g", "z4_g", "tya_g")


def chain_body(scalars, start, get, res, scr, sem):
    level, wide = here()
    start(FIRST)
    land = {n: scr["land_" + n] for n in LANDS}
    corner = scalars["well_x"][level]
    rows_at = scalars["well_y"][level]
    barrier, count = greet()
    kg, kf = scr["kg"], scr["kf"]
    features(FY, PF, FZ * 4, get("x_in_f"), get("z4_f")[...], get("tya_f")[...], scr["feat_f"], kf, scr["x_ff"])
    features(YG, PG, GZ * 4, get("x_in_g"), get("z4_g")[...], get("tya_g")[...], scr["feat_g"], kg, scr["x_g"])
    pl.semaphore_wait(barrier, count)

    push_level(lambda peer: kg.at[pl.ds(8 * peer, 8)], land["in_level"], sem["in_level"])
    start(CHAIN_INPUTS)
    land["in_level"][level] = kg[pl.ds(8 * level, 8)]
    msg = scr["msg_in"]
    msg[...] = jnp.zeros(msg.shape, F32)
    for w in range(WD):
        msg[w, PG : PG + PF, :] = kf[w // 2]
    finish(land["in_level"], sem["in_level"], LV)
    total = land["in_level"][0] + land["in_level"][1] + land["in_level"][2] + land["in_level"][3]
    for w in range(WD):
        msg[w, :PG, :] = total[w // 8]
    push_wide(lambda peer: msg.at[peer], land["in"], sem["in"])
    land["in"][wide] = msg[wide]
    tile = get("tile")[...]
    lift_g, lift_f = get("lift_g")[...].astype(F32), get("lift_f")[...].astype(F32)
    point_g = mmh(lift_g, get("mix_g")[...].astype(F32))
    point_f = mmh(lift_f, get("mix_f")[...].astype(F32))
    ro_g, ro_f = get("ro_g")[...].astype(F32), get("ro_f")[...].astype(F32)
    spread, fold = get("spread"), get("fold")[...]
    lift_lanes = mm(get("lift_f")[...], spread[...])[4:5, :]
    for b in range(NB):
        scr["lm_g"][b] = point_block(point_g, b, tile, 2)[: GZ * 4]
    w_f, w_g = get("w_f"), get("w_g")
    acc = scr["mix_a"]
    for c in range(CC // CHUNK):
        part = weights_chunk(w_f, c) * lift_lanes[:, CHUNK * c : CHUNK * (c + 1)]
        if c == 0:
            acc[...] = part
        else:
            acc[...] += part
    scr["v_f"][...] = mm_split(acc[...], fold)
    finish(land["in"], sem["in"], WD)

    u = halves(land["in"][...].reshape(WD * 8, 128))
    s = mmh(mmh(get("txs_g")[...], u), selector(lift_g, 2, 2 * lax.rem(wide, 8), 4))
    p_gm = scr["p_gm"]
    p_gm[...] = mix_modes(s, 2, w_g, spread, fold, get("txb_g")[...], scr["mix_ga"], scr["mix_gb"]).reshape(p_gm.shape)
    push_wide(lambda peer: p_gm.at[peer], land["g"], sem["g"])
    land["g"][wide] = p_gm[wide]
    res["s_g"][...] = s
    first = 8 * lax.rem(wide, 2)
    s_f = mmh(mmh(get("txs_f")[...], u), selector(lift_f[:4], 8, first, 4))
    sel_c = selector(lift_f[4:5], 8, first, 1)
    for b in range(NB):
        scr["lm_f"][b] = point_block(point_f[:4], b, tile, 2)
        scr["lc_f"][b] = point_block(point_f[4:5], b, tile, 0)
    finish(land["g"], sem["g"], WD)
    land["g_level"][level] = land["g"][...].reshape(WD * 8, 128).astype(BF)
    push_level(lambda peer: land["g_level"].at[level], land["g_level"], sem["g_level"])
    cot_in = get("cot_in_f")
    for y in range(FY):
        scr["cot_f"][PF * y : PF * (y + 1), :] = cot_in[:, FZ * y : FZ * (y + 1)]
    ones_cl = get("ones_cl")[...]
    scr["wide_cot"][...] = mm_split(scr["cot_f"][...], ones_cl)
    cot, cot_in = scr["cot"], get("cot_in_g")
    cot[...] = jnp.zeros(cot.shape, F32)
    for y in range(YG):
        cot[PG * y : PG * (y + 1), :GZ] = cot_in[:, GZ * y : GZ * (y + 1)]
    finish(land["g_level"], sem["g_level"], LV)

    scr["x_wide"][...] = land["g_level"][...].astype(F32).reshape(KF, 8, 8, 128)
    for q in range(8):
        scr["x_in"][:, 128 * q : 128 * (q + 1)] = scr["x_wide"][:, q].reshape(256, 128).astype(BF)
    perm_in = get("perm_in")[...]
    bb = mm(get("tyi_g")[...], mm(scr["x_in"][...], perm_in).astype(BF)).astype(BF)
    zi = get("zi_g")[...]
    acc, acc_pt = scr["acc"], scr["acc_pt"]
    for b in range(NB):
        pre = block_pre(bb, b, zi) + mm(scr["feat_g"][...], scr["lm_g"][b])
        hidden, slope = gelu_parts(pre)
        scr["slope"][b] = slope.astype(BF)
        part = hidden * lanes_of(ro_g, b, tile)
        if b == 0:
            acc[...] = part
        else:
            acc[...] += part
    sum_cl = get("sum_cl")[...]
    pred = mm_split(acc[...], sum_cl).astype(BF)
    scr["pred_b"][...] = pred
    push_level(lambda peer: scr["pred_b"], land["rows"], sem["rows"])
    land["rows"][level] = pred
    res["pred_g"][...] = pred.astype(F32)
    pick_box = shift_rows(256, LV * 256, 8 * PG * rows_at).astype(BF)
    finish(land["rows"], sem["rows"], LV)

    box = mm(pick_box, land["rows"][...].reshape(LV * 256, ZP))
    a = mmh(box, get("zc")[...])
    scr["s_box"][...] = mmh(get("tya_box")[...], halves(a))
    for p in range(PG):
        for r in range(2):
            at = 2 * MODES * p + MODES * r
            scr["o_box"][:, at : at + MODES] = scr["s_box"][pl.ds(KF * PG * r + p, KF, stride=PG), :]
    spec_m, planes_m = scr["spec_m"], scr["planes_m"]
    spec_m[...] = scr["o_box"][...].reshape(spec_m.shape)
    push_wide(lambda peer: spec_m.at[peer // 2], land["spec"], sem["spec"])
    land["spec"][wide] = spec_m[wide // 2]
    scr["box_f"][...] = box
    planes = [pair_rows(scr["box_f"], p, PG, FY // 4) for p in range(PG)]
    for r in range(PG):
        mine_r = lax.rem(corner + r, PG)
        which = jnp.zeros((32, 128), jnp.int32) + mine_r
        planes_m[r] = sum(jnp.where(which == p, planes[p], 0.0) for p in range(PG)).astype(BF)
    push_wide(lambda peer: planes_m.at[peer % PG], land["box"], sem["box"])
    land["box"][wide] = planes_m[wide % PG]
    pick_x = shift_rows(FX // 2, GX, corner)
    finish(land["spec"], sem["spec"], WD)

    got = land["spec"][...].reshape(WD, 128)
    for p in range(PG):
        scr["x_box"][pl.ds(p, WD, stride=PG), :] = got[:, 2 * MODES * p : 2 * MODES * (p + 1)]
    box = mmh(pick_x, scr["x_box"][...])
    s_f = s_f + mmh(mmh(get("txs_box")[...], halves(box)), sel_c)
    p_f, p_fm = scr["p_f"], scr["p_fm"]
    value = mix_modes(s_f, 8, w_f, spread, fold, get("txb_f")[...], scr["mix_a"], scr["mix_b"])
    for k in range(4):
        p_f[pl.ds(k, 2 * FX, stride=4), :] = value[:, 128 * k : 128 * (k + 1)]
    p_fm[...] = p_f[...].astype(BF).reshape(p_fm.shape)
    push_wide(lambda peer: p_fm.at[peer], land["f"], sem["f"])
    land["f"][wide] = p_fm[wide]
    res["s_f"][...] = s_f
    finish(land["box"], sem["box"], WD)
    plane = pick_plane(land["box"][...].astype(F32), lax.div(corner + wide, PG)).astype(BF)
    rows_up = get("rows_up")
    rows = mm(rows_up[0], plane[:, :ZP]) + mm(rows_up[1], plane[:, ZP:])
    cl = mm(rows.astype(BF), get("z_up")[...]).astype(BF)
    finish(land["f"], sem["f"], WD)

    scr["x_f"][...] = land["f"][...].astype(F32).reshape(KF, 32, 128)
    for g in range(8):
        lanes = scr["x_f"][:, pl.ds(16 * (g // 4) + g % 4, 4, stride=4), :]
        scr["x_fb"][:, 128 * g : 128 * (g + 1)] = lanes.reshape(128, 128).astype(BF)
    bb = mm(get("tyi_f")[...], mm(scr["x_fb"][...], perm_in).astype(BF)).astype(BF)
    zi, zf = get("zi_f")[...], get("zf_f")[...]
    for b in range(NB):
        pre = block_pre(bb, b, zi) + mm(scr["feat_f"][...], scr["lm_f"][b]) + mm(cl, scr["lc_f"][b])
        hidden, slope = gelu_parts(pre)
        ro_lanes = lanes_of(ro_f, b, tile)
        gp = (slope * (scr["wide_cot"][...] * ro_lanes)).astype(BF)
        part = hidden * ro_lanes
        part_pt = gp.astype(F32) * lanes_of(point_f[4:5], b, tile)
        if b == 0:
            acc[...] = part
            acc_pt[...] = part_pt
        else:
            acc[...] += part
            acc_pt[...] += part_pt
        put_block(scr["a"], gp, b, zf)
    z = forward_tail(scr["a"], get("tyf_f")[...], get("perm_wide")[...])
    m_f, m_fm = scr["m_f"], scr["m_fm"]
    for g in range(8):
        m_f[:, pl.ds(16 * (g // 4) + g % 4, 4, stride=4), :] = z[:, 128 * g : 128 * (g + 1)].reshape(KF, 4, 128)
    m_fm[...] = m_f[...].astype(BF).reshape(m_fm.shape)
    push_wide(lambda peer: m_fm.at[peer], land["dual"], sem["dual"])
    land["dual"][wide] = m_fm[wide]
    point = mm_split(acc_pt[...], sum_cl)
    scr["pt"][...] = mmh(mmh(get("rows_down")[...], point), get("z_down")[...])
    pt_m = scr["pt_m"]
    pt_m[...] = pair_rows(scr["pt"], 0, 1, FY // 4).astype(BF)
    push_wide(lambda peer: pt_m, land["pts"], sem["pts"])
    land["pts"][wide] = pt_m[...]
    res["pred_f"][...] = mm_split(acc[...], sum_cl)
    place_x = shift_rows(2 * GX, FX, -2 * corner)
    finish(land["dual"], sem["dual"], WD)

    d_f, d_lanes = scr["d_f"], scr["d_lanes"]
    d_f[...] = land["dual"][...].astype(F32).reshape(d_f.shape)
    for g in range(4):
        d_lanes[:, 128 * g : 128 * (g + 1)] = d_f[pl.ds(g, 2 * FX, stride=4), :].astype(BF)
    z = mm(get("txd_f")[...], d_lanes[...])
    rows = 2 * KF
    zc, zd = z[2 * rows : 3 * rows], z[3 * rows :]
    cols = []
    for m in range(8):
        v = scr["v_f"][rows * m : rows * (m + 1), :]
        lanes = slice(lane_f(m), lane_f(m) + CH)
        cols.append(jnp.concatenate([
            jnp.sum(v * zc[:, lanes], axis=1, keepdims=True),
            jnp.sum(v * zd[:, lanes], axis=1, keepdims=True)], axis=0))
    q_rows, q_m = scr["q_rows"], scr["q_m"]
    q_rows[...] = mmh(place_x, mmh(get("txb_box")[...], jnp.concatenate(cols, axis=1)))
    lanes = [q_rows[pl.ds(r, WD, stride=8), :] for r in range(8)]
    lanes.append(jnp.zeros((WD, 64), F32))
    q_m[...] = jnp.concatenate(lanes, axis=1).reshape(q_m.shape)
    own = land["q"].at[level]
    push_wide(lambda peer: q_m.at[peer], own, sem["q"])
    own[wide] = q_m[wide]
    res["dual_f"][...] = z[: 2 * rows].astype(BF)
    finish(land["pts"], sem["pts"], WD)
    mine = scr["mine"]
    planes = land["pts"][...].astype(F32)
    for p in range(PG):
        mine[32 * p : 32 * (p + 1), :] = pick_plane(planes, PG * wide + p - corner).astype(BF)
    push_level(lambda peer: mine, land["pt_level"], sem["pt_level"])
    land["pt_level"][level] = mine[...]
    finish(own, sem["q"], WD)
    push_level(lambda peer: own, land["q"], sem["q_level"])
    tyb = get("tyb_box")[...]
    tables = []
    for l in range(LV):
        tables.append(mm(shift_rows(YG, FY // 2, YG * level - 8 * scalars["well_y"][l]).astype(BF), tyb).astype(BF))
    finish(land["pt_level"], sem["pt_level"], LV)
    planes = jnp.zeros((128, 128), F32)
    for l in range(LV):
        move = shift_rows(128, 128, 32 * level - 4 * scalars["well_y"][l], 32).astype(BF)
        planes += mm(move, land["pt_level"][l])
    for p in range(PG):
        for k in range(2):
            part = planes[32 * p : 32 * (p + 1), ZP * k : ZP * (k + 1)]
            cot[pl.ds(PG * k + p, 32, stride=2 * PG), :] += part
    finish(land["q"], sem["q_level"], LV)

    q = land["q"][...].reshape(LV * WD, 128)[:, :64]
    odd = jnp.bitwise_and(lax.broadcasted_iota(jnp.int32, q.shape, 0), 1) == 1
    q = jnp.concatenate([jnp.where(odd, 0.0, q), jnp.where(odd, q, 0.0)], axis=1).astype(BF)
    g = mm(q, get("dd_box")[...]).astype(BF)
    total = jnp.zeros((YG, PG * ZP), F32)
    for l in range(LV):
        part = g[WD * l : WD * (l + 1)]
        part = jnp.concatenate([part[:, PG * ZP * k : PG * ZP * (k + 1)] for k in range(4)], axis=0)
        total += mm(tables[l], part)
    for p in range(PG):
        cot[pl.ds(p, YG, stride=PG), :] += total[:, ZP * p : ZP * (p + 1)]
    wide_cot = mm_split(cot[...], ones_cl)
    zf = get("zf_g")[...]
    for b in range(NB):
        gp = (scr["slope"][b].astype(F32) * (wide_cot * lanes_of(ro_g, b, tile))).astype(BF)
        put_block(scr["a"], gp, b, zf)
    send_g = scr["send_g"]
    send_g[...] = forward_tail(scr["a"], get("tyf_g")[...], get("perm_out")[...]).astype(BF).reshape(send_g.shape)
    push_level(lambda peer: send_g.at[peer], land["out_level"], sem["out_level"])
    land["out_level"][level] = send_g[level]
    msg = scr["msg_out"]
    msg[...] = jnp.zeros(msg.shape, F32)
    finish(land["out_level"], sem["out_level"], LV)
    out = land["out_level"]
    total = out[0].astype(F32) + out[1].astype(F32) + out[2].astype(F32) + out[3].astype(F32)
    for q in range(8):
        msg[:, q, :, : 2 * CH] = total[:, 2 * CH * q : 2 * CH * (q + 1)].reshape(8, 8, 2 * CH)
    push_wide(lambda peer: msg.at[peer // 8, peer % 8], res["got_g"], sem["got_g"])
    res["got_g"][wide] = msg[wide // 8, wide % 8]
    finish(res["got_g"], sem["got_g"], WD)


def last_body(scalars, start, get, res, scr, sem):
    start(LAST_INPUTS)
    spread, tile_out = get("spread"), get("tile_out")[...]
    rows = 2 * KF
    done = []

    def send(src, dst, k):
        copy = pltpu.make_async_copy(src, dst, sem["out"].at[k])
        copy.start()
        done.append(copy)

    def grads(s, za, zb, modes, buf):
        sa, sb = stack_modes(s[:rows], modes, lane_g), stack_modes(s[rows:], modes, lane_g)

        def put(lanes, value):
            buf[:, :, :, lanes] = value

        grad_modes(sa, sb, mm(za, tile_out), mm(zb, tile_out), spread, put)

    s_f, d_f = get("s_f")[...], get("dual_f")[...]
    for k in range(2):
        buf = scr["gf"].at[pl.ds(4 * k, 4)]
        d = d_f[:, 256 * k : 256 * (k + 1)]
        grads(s_f[:, 4 * CH * k : 4 * CH * (k + 1)], stack_modes(d[:rows], 4, lane_f), stack_modes(d[rows:], 4, lane_f), 4, buf)
        send(buf, res["grad_f"].at[pl.ds(4 * k, 4)], k)
    z = mm(get("txd_g")[...], get("got_g")[...].reshape(2 * GX, 128).astype(BF))
    grads(get("s_g")[...], stack_modes(z[:rows], 2, lane_f), stack_modes(z[rows:], 2, lane_f), 2, res["grad_g"])
    pred = get("pred_g")
    for y in range(YG):
        scr["out_g"][:, GZ * y : GZ * (y + 1)] = pred[PG * y : PG * (y + 1), :GZ]
    res["coarse"][...] = scr["out_g"][...].astype(BF)
    pred = get("pred_f")
    for y in range(FY):
        scr["out_f"][:, FZ * y : FZ * (y + 1)] = pred[PF * y : PF * (y + 1), :]
    res["fine"][0] = scr["out_f"][...].astype(BF)
    for copy in done:
        copy.wait()


CHAIN_TABLES = {
    "z4_f": Z4_F, "tya_f": TYA_F, "z4_g": Z4_G, "tya_g": TYA_G,
    "tile": TILE_CL, "spread": SPREAD_IN, "fold": FOLD, "txs_g": TXS_G, "txb_g": TXB_G, "txs_f": TXS_F,
    "ones_cl": ONES_CL, "perm_in": PERM_WIDE, "tyi_g": TYI_G, "zi_g": ZI_G, "sum_cl": SUM_CL, "zc": ZC,
    "tya_box": TYA_BOX, "txs_box": TXS_BOX, "txb_f": TXB_F, "rows_up": ROWS_UP, "z_up": Z_UP, "tyi_f": TYI_F,
    "zi_f": ZI_F, "zf_f": ZF_F, "tyf_f": TYF_F, "perm_wide": PERM_WIDE_OUT, "rows_down": ROWS_DOWN, "z_down": Z_DOWN,
    "txd_f": TXD_F, "txb_box": TXB_BOX, "tyb_box": TYB_BOX, "dd_box": DD_BOX, "zf_g": ZF_G, "tyf_g": TYF_G,
    "perm_out": PERM_OUT,
}
CHAIN_PARAMS = ("lift_g", "lift_f", "mix_g", "mix_f", "ro_g", "ro_f", "w_f", "w_g", "cot_in_f", "cot_in_g")
CHAIN_INPUTS = (*CHAIN_PARAMS, *CHAIN_TABLES)
LAST_INPUTS = ("spread", "tile_out", "s_f", "dual_f", "txd_g", "got_g", "s_g", "pred_g", "pred_f")


def shards(coarse_input, fine_input, coarse_cotangent, fine_cotangent, well_x, well_y, coarse_lift, coarse_mixing,
           coarse_spectral, coarse_readout, fine_lift, fine_mixing, fine_spectral, fine_readout):
    inputs = {
        "x_in_f": fine_input[0], "x_in_g": coarse_input, "lift_g": coarse_lift, "lift_f": fine_lift[0],
        "mix_g": coarse_mixing, "mix_f": fine_mixing[0], "ro_g": coarse_readout[None], "ro_f": fine_readout,
        "w_f": fine_spectral[0], "w_g": coarse_spectral, "cot_in_f": fine_cotangent[0], "cot_in_g": coarse_cotangent,
    }
    inputs.update({n: jnp.asarray(t) for n, t in CHAIN_TABLES.items()})
    scratch = {**{"land_" + n: v for n, v in LANDS.items()}, **SCRATCH}
    res = run(chain_body, RESULTS, {"well_x": well_x, "well_y": well_y}, inputs, scratch, SEMS, cid=1, name="chain")
    inputs = {n: res[n] for n in ("s_f", "dual_f", "got_g", "s_g", "pred_g", "pred_f")}
    inputs.update(spread=jnp.asarray(SPREAD_IN), tile_out=jnp.asarray(TILE_OUT), txd_g=jnp.asarray(TXD_G))
    out = run(
        last_body,
        {"grad_g": ((2, KF, 2, CC), F32), "grad_f": ((8, KF, 2, CC), F32), "coarse": ((PG, YG * GZ), BF),
         "fine": ((1, PF, FY * FZ), BF)},
        {}, inputs,
        {"gf": ((8, KF, 2, CC), F32), "out_g": ((PG, YG * GZ), F32), "out_f": ((PF, FY * FZ), F32)},
        ("out",), kept=("grad_f",), name="last")
    return out["coarse"], out["fine"], out["grad_g"], out["grad_f"][None]


def solution(mesh):
    placed = (
        P("wide", "level"),
        P("level", "wide", None),
        P("wide", "level"),
        P("level", "wide", None),
        P(),
        P(),
        P(),
        P(),
        P(("level", "wide"), None, None, None),
        P(),
        P("level", None, None),
        P("level", None, None),
        P("level", "wide", None, None, None),
        P("level", None),
    )
    return jax.shard_map(
        shards,
        mesh=mesh,
        in_specs=placed,
        out_specs=(
            P("wide", "level"),
            P("level", "wide", None),
            P(("level", "wide"), None, None, None),
            P("level", "wide", None, None, None),
        ),
        check_vma=False,
    )
```

time: 222 us -> 139 us (0.63)
  Pallas kernels: 198 us -> 138 us
  local copies, waits for them, and re-layouts: 21 us -> 0 us
    pallas_call x19 -> x2, Pallas kernels: 198 us -> 138 us  [run(): pl.pallas_call(kernel, out_shape=[jax.ShapeDtypeStruct(s, d) for s, d in...]
    unnamed x118 -> x0, local copies, waits for them, and re-layouts: 14.7 us -> none
    reshape x4 -> x0, local copies, waits for them, and re-layouts: 2.98 us -> none  [the longest x2 2.2 us: shards(): pred_f.reshape(FY, PF, FZ).transpose(1, 0, 2).reshape(1, PF, FY * FZ)]
    dynamic_slice x2 -> x0, local copies, waits for them, and re-layouts: 2.56 us -> none  [the longest x1 1.31 us: shards(): well_y[level]]
where the time goes in v2:
time: 139 us
  Pallas kernels  138 us (99%)
    pallas_call x2, Pallas kernels, run(): pl.pallas_call(kernel, out_shape=[jax.ShapeDtypeStruct(s, d) for s, d in...  138 us

profile of v2, /device:TPU:1, one launch (start us, length us, event | category | flops | bytes accessed | tf_op | source)
XLA Modules:
  0.0 139.2 jit_solution(3000234813836649012)
XLA Ops:
  0.6 132.9 %chain.1 = (f32[256,64]{1,0:T(8,128)}, f32[256,64]{1,0:T(8,128)}, f32[128,96]{1,0:T(8,128)}, f32[128,384]{1,0:T(8,128)}, bf16[128,512]{1,0:T(8,128)(2,1)}, /*index=5*/f32[64,8,128]{2,1,0:T(8,128)}) custom-call(s32[4]{0:T(128)} %refs_0_.1, s32[4]{0:T(128)} %refs_1_.1, bf16[2,32768]{1,0:T(2,128)(2,1)} %bitcast.8, bf16[4,12800]{1,0:T(4,128)(2,1)} %refs_3_.1, ...), custom_call_target="tpu_custom_call" | custom-call | tf_op jit(solution)/shard_map/chain/pallas_call | solution.py:222
  133.5 5.5 %last.1 = (f32[2,32,2,2304]{3,2,1,0:T(2,128)}, f32[8,32,2,2304]{3,2,1,0:T(2,128)}, bf16[4,3200]{1,0:T(4,128)(2,1)}, bf16[1,2,8192]{2,1,0:T(2,128)(2,1)}) custom-call(f32[128,384]{1,0:T(8,128)} %get-tuple-element.14.refs_0_, bf16[128,512]{1,0:T(8,128)(2,1)} %get-tuple-element.15.refs_1_, f32[64,8,128]{2,1,0:T(8,128)} %get-tuple-element.16.refs_2_, ...), custom_call_target="tpu_custom_call" | custom-call | tf_op jit(solution)/shard_map/last/pallas_call | solution.py:222

commit v3 on v2

v3 whole, which is shorter than its diff:
```python
import math
from types import SimpleNamespace as Names

import ml_dtypes
import numpy as np
import jax
import jax.numpy as jnp
from jax import lax
from jax.experimental import pallas as pl
from jax.experimental.pallas import tpu as pltpu
from jax.sharding import PartitionSpec as P

MODES = 16
KF = 2 * MODES
CH = 48
NB = 6
CL = 8
GX = 256
GY = 256
GZ = 50
FX = 128
FY = 128
FZ = 64
ZP = 64
LV = 4
WD = 64
PG = 4
YG = 64
PF = 2
CC = CH * CH
BF = jnp.bfloat16
F32 = jnp.float32
HIGH = lax.Precision.HIGHEST
VMEM_BYTES = 60 * 2**20


def bf(x):
    return np.asarray(x, np.float32).astype(ml_dtypes.bfloat16)


def f32(x):
    return np.asarray(x, np.float32)


def waves(rows, length):
    j = np.arange(KF)
    signed = np.where(j < MODES, j, j - KF)
    turn = np.mod(rows[:, None] * signed[None, :], length) * (2.0 * math.pi / length)
    return np.cos(turn) / math.sqrt(length), np.sin(turn) / math.sqrt(length)


def forward_table(rows, length):
    c, s = waves(rows, length)
    c, s = c.T, s.T
    return np.stack([np.stack([c, s], 1), np.stack([-s, c], 1)], 0)


def depth(length):
    c, s = waves(np.arange(length), length)
    both = np.stack([c[:, :MODES], -s[:, :MODES]], 1)
    both = bf(both).astype(np.float64)
    return np.concatenate([both, np.zeros((ZP - length, 2, MODES))], 0)


D_G, D_F = depth(GZ), depth(FZ)
ZMAP = np.zeros((ZP, FZ))
ZMAP[np.arange(FZ) * GZ // FZ, np.arange(FZ)] = 1.0
D_POOL = np.einsum("gf,frk->grk", ZMAP, D_F)


def depth_blocks(d):
    return np.einsum("zrk,ij->zirkj", d, np.eye(CL)).reshape(ZP * CL, 2 * MODES * CL)


def depth_features(d, length):
    return np.einsum("zrk,ij->zirkj", d[:length], np.eye(4)).reshape(length * 4, 2 * MODES * 4)


ZF_G, ZF_F = bf(depth_blocks(D_G)), bf(depth_blocks(D_F))
ZI_G, ZI_F = bf(depth_blocks(D_G).T), bf(depth_blocks(D_F).T)
Z4_G, Z4_F = bf(depth_features(D_G, GZ)), bf(depth_features(D_F, FZ))
ZC = f32(D_POOL.reshape(ZP, 2 * MODES))

FY_G = np.stack([forward_table(v * YG + np.arange(YG), GY) for v in range(LV)], 0)
FY_F = forward_table(np.arange(FY), FY)
FY_BOX = FY_F.reshape(2, KF, 2, FY // 2, 2).sum(4)
FX_G = forward_table(np.arange(GX), GX)
FX_F = forward_table(np.arange(FX), FX)
FX_BOX = FX_F.reshape(2, KF, 2, FX // 2, 2).sum(4)
EYE_G, EYE_F = np.eye(PG), np.eye(PF)

TYA_G = f32(np.einsum("vakbt,pq->vakpbtq", FY_G, EYE_G).reshape(LV, 2 * KF * PG, 2 * YG * PG))
TYA_F = f32(np.einsum("akbt,pq->akpbtq", FY_F, EYE_F).reshape(2 * KF * PF, 2 * FY * PF))
TYA_BOX = f32(np.einsum("akbt,pq->akpbtq", FY_BOX, EYE_G).reshape(2 * KF * PG, FY * PG))
TYF_G = bf(np.einsum("vakbt,pq->vkpabtq", FY_G, EYE_G).reshape(LV, KF * PG * 2, 2 * YG * PG))
TYF_F = bf(np.einsum("akbt,pq->kpabtq", FY_F, EYE_F).reshape(KF * PF * 2, 2 * FY * PF))
TYI_G = bf(np.einsum("vbkat,pq->vatpkqb", FY_G, EYE_G).reshape(LV, 2 * YG * PG, KF * PG * 2))
TYI_F = bf(np.einsum("bkat,pq->atpkqb", FY_F, EYE_F).reshape(2 * FY * PF, KF * PF * 2))
TYB_BOX = bf(np.repeat(FY_BOX.transpose(3, 2, 0, 1).reshape(FY // 2, 4 * KF), 2, axis=1))
DD_BOX = bf(np.einsum("zahk,pq,rs->hprkasqz", D_POOL.reshape(ZP, 2, 2, 8), EYE_G, np.eye(2)).reshape(128, 4 * PG * ZP))


def source_rows(table):
    a = np.stack([table[0], -table[1]], 1)
    b = np.stack([table[1], table[0]], 1)
    return np.stack([a, b], 0).reshape(4 * KF, 2, -1)


def in_rows(table, planes, first):
    rows = source_rows(table).reshape(4 * KF, 2, WD, planes)
    out = np.zeros((4 * KF, 2, WD, 8))
    out[..., first : first + planes] = rows
    return out.reshape(4 * KF, 2 * WD * 8)


TXS_G = f32(in_rows(FX_G, PG, 0))
TXS_F = f32(in_rows(FX_F, PF, PG))
TXS_BOX = f32(source_rows(FX_BOX).reshape(4 * KF, FX))


def dual_rows(table, count):
    r, i = table[0], table[1]
    kinds = [np.stack([r, r], 1), np.stack([i, i], 1), np.stack([r, i], 1), np.stack([i, -r], 1)]
    rows = np.stack(kinds[:count], 0).transpose(0, 1, 2, 4, 3)
    return rows.reshape(count * 2 * KF, -1)


TXD_G = bf(dual_rows(FX_G, 2))
TXD_F = bf(dual_rows(FX_F, 4))


def back_rows(table):
    back = table.transpose(3, 2, 0, 1)
    back = np.stack([back, back], 4)
    return back.reshape(back.shape[0] * 2, 4 * KF)


TXB_G = bf(back_rows(FX_G))
TXB_F = bf(back_rows(FX_F))
TXB_BOX = f32(back_rows(FX_BOX))

PERM = np.zeros((MODES, NB, CL, NB, MODES, CL))
for _k in range(MODES):
    for _b in range(NB):
        for _l in range(CL):
            PERM[_k, _b, _l, _b, _k, _l] = 1.0
PERM = PERM.reshape(MODES * CH, MODES * CH)
PERM_OUT = bf(PERM.T)
PERM_WIDE = np.zeros((8, 128, MODES * CH))
PERM_WIDE[:, : 2 * CH] = PERM.reshape(8, 2 * CH, MODES * CH)
PERM_WIDE = PERM_WIDE.reshape(1024, MODES * CH)
PERM_WIDE, PERM_WIDE_OUT = bf(PERM_WIDE), bf(PERM_WIDE.T)
SPREAD_IN = bf(np.kron(np.eye(CH), np.ones((1, CH))))
CHUNK = 8 * CH
TILE_OUT = bf(np.kron(np.ones((1, 8)), np.eye(CH)))
FOLD = bf(np.kron(np.ones((8, 1)), np.eye(CH)))
ONES_CL = bf(np.kron(np.eye(ZP), np.ones((1, CL))))
SUM_CL = bf(np.kron(np.eye(ZP), np.ones((CL, 1))))
TILE_CL = f32(np.kron(np.ones((1, ZP)), np.eye(CL)))
ROWS_UP = np.kron(np.eye(FY // 2), np.ones((2 * PF, 1))).reshape(256, FY // 4, 2).transpose(2, 0, 1)
ROWS_UP = bf(ROWS_UP)
ROWS_DOWN = f32(np.kron(np.eye(FY // 2), np.ones((1, 2 * PF))))
Z_UP = bf(ZMAP)
Z_DOWN = f32(ZMAP.T)


def mm(a, b):
    return jnp.dot(a, b, preferred_element_type=F32)


def mmh(a, b):
    return jnp.dot(a, b, preferred_element_type=F32, precision=HIGH)


MESH = pl.DeviceIdType.MESH
DMA2 = pltpu.SemaphoreType.DMA((2,))


def vm(shape, kind=F32):
    return pltpu.VMEM(shape, kind)


BY_LEVEL = dict(tya_g=LV, tyi_g=LV, tyf_g=LV)


def run(body, outs, smem, inputs, scratch, sems={}, kept=0, passed=(), cid=None, name=None):
    held = {n: vm(t.shape[1:] if n in BY_LEVEL else t.shape, t.dtype) for n, t in inputs.items() if n not in passed}

    def kernel(*refs):
        refs = list(refs)

        def take(names):
            got = {n: refs.pop(0) for n in names}
            return got

        scalars = take(smem)
        given = take(inputs)
        res = take(outs)
        scr = take(scratch)
        sem = take(sems)
        inside = take(held)
        load_sem = refs.pop(0)
        level = lax.axis_index("level")
        copies, started, ready = {}, set(), set()
        for k, n in enumerate(held):
            src = given[n].at[level] if n in BY_LEVEL else given[n]
            copies[n] = pltpu.make_async_copy(src, inside[n], load_sem.at[k])

        def start(count):
            for n in list(copies)[:count]:
                if n not in started:
                    copies[n].start()
                    started.add(n)

        class Get:
            def __getattr__(self, n):
                if n in passed:
                    return given[n]
                if n not in ready:
                    copies[n].wait()
                    ready.add(n)
                return inside[n]

        body(Names(**scalars), start, Get(), Names(**res), Names(**scr), Names(**sem))

    got = pl.pallas_call(
        kernel,
        out_shape=[jax.ShapeDtypeStruct(s, d) for s, d in outs.values()],
        in_specs=[pl.BlockSpec(memory_space=pltpu.SMEM)] * len(smem) + [pl.BlockSpec(memory_space=pl.ANY)] * len(inputs),
        out_specs=[pl.BlockSpec(memory_space=pl.ANY if k < kept else pltpu.VMEM) for k in range(len(outs))],
        scratch_shapes=[pltpu.SemaphoreType.DMA((v,)) if v == 4 else vm(*v) for v in scratch.values()] + [DMA2] * len(sems) + list(held.values())
        + [pltpu.SemaphoreType.DMA((len(held),))],
        name=name,
        compiler_params=pltpu.CompilerParams(
            vmem_limit_bytes=VMEM_BYTES, collective_id=cid, has_side_effects=cid is not None),
    )(*smem.values(), *inputs.values())
    return Names(**dict(zip(outs, got)))


def halves(u):
    half = u.shape[1] // 2
    return jnp.concatenate([u[:, :half], u[:, half:]], axis=0)


def features(rows, planes, width, x_ref, z, table, feat_ref, out_ref, scr):
    for y in range(rows):
        scr[planes * y : planes * (y + 1), :] = x_ref[:, width * y : width * (y + 1)].astype(F32)
    feat = scr[...].astype(BF)
    feat_ref[...] = feat
    both = mmh(table, halves(mm(feat, z)))
    rows_out = both.shape[0] // 2
    lanes = jnp.concatenate([both[:rows_out], both[rows_out:]], axis=1)
    out_ref[...] = lanes.reshape(out_ref.shape)


def lanes_of_modes(shape):
    lane = lax.broadcasted_iota(jnp.int32, shape, 1)
    inside = jnp.bitwise_and(lane, 127)
    mode = 2 * lax.shift_right_logical(lane, 7) + (inside >= CH).astype(jnp.int32)
    return jnp.where(inside < 2 * CH, mode, 8 + MODES)


def stack_modes(x, modes, lane):
    return jnp.concatenate([x[:, lane(m) : lane(m) + CH] for m in range(modes)], axis=0)


def lane_g(m):
    return CH * m


def lane_f(m):
    return 128 * (m // 2) + CH * (m % 2)


def weights_chunk(w_ref, c):
    w = w_ref[:, :, :, CHUNK * c : CHUNK * (c + 1)].astype(F32)
    return w.reshape(w.shape[0] * 2 * KF, CHUNK)


def mix_modes(s, modes, w_ref, spread, fold, table, acc_a, acc_b):
    half = 2 * KF
    sa, sb = stack_modes(s[:half], modes, lane_g), stack_modes(s[half:], modes, lane_g)
    for c in range(CC // CHUNK):
        w = weights_chunk(w_ref, c)
        e = spread[:, CHUNK * c : CHUNK * (c + 1)]
        if c == 0:
            acc_a[...] = w * mm_split(sa, e)
            acc_b[...] = w * mm_split(sb, e)
        else:
            acc_a[...] += w * mm_split(sa, e)
            acc_b[...] += w * mm_split(sb, e)
    pa, pb = mm_split(acc_a[...], fold), mm_split(acc_b[...], fold)
    spare = jnp.zeros((2 * half, 128 - 2 * CH), F32)
    parts = []
    for m in range(modes):
        parts.append(jnp.concatenate([pa[half * m : half * (m + 1)], pb[half * m : half * (m + 1)]], axis=0))
        if m % 2 == 1:
            parts.append(spare)
    return mm_split_right(table, jnp.concatenate(parts, axis=1))


def grad_modes(sa, sb, za, zb, spread, put):
    for c in range(CC // CHUNK):
        e = spread[:, CHUNK * c : CHUNK * (c + 1)]
        g = mm_split(sa, e) * za + mm_split(sb, e) * zb
        put(slice(CHUNK * c, CHUNK * (c + 1)), g.reshape(g.shape[0] // (2 * KF), KF, 2, CHUNK))


def grads(s, za, zb, modes, spread, tile_out, buf):
    rows = 2 * KF
    sa, sb = stack_modes(s[:rows], modes, lane_g), stack_modes(s[rows:], modes, lane_g)

    def put(lanes, value):
        buf[:, :, :, lanes] = value

    grad_modes(sa, sb, mm_split(za, tile_out), mm_split(zb, tile_out), spread, put)


def shift_rows(rows, cols, by, group_rows=None):
    r = lax.broadcasted_iota(jnp.int32, (rows, cols), 0)
    c = lax.broadcasted_iota(jnp.int32, (rows, cols), 1)
    hit = c - r == by
    if group_rows is not None:
        shift = group_rows.bit_length() - 1
        hit = jnp.logical_and(hit, lax.shift_right_logical(r, shift) == lax.shift_right_logical(c, shift))
    return jnp.where(hit, 1.0, 0.0)


def pick_packed(by, half):
    r = lax.broadcasted_iota(jnp.int32, (256, LV * 128), 0)
    c = lax.broadcasted_iota(jnp.int32, (256, LV * 128), 1)
    row = 256 * lax.shift_right_logical(c, 7) + jnp.bitwise_and(c, 127) + 128 * half
    return jnp.where(row - r == by, 1.0, 0.0).astype(BF)


def where_at(which, at, planes):
    return jnp.where(which == at, planes, 0.0)


def pick_plane(planes, at):
    which = lax.broadcasted_iota(jnp.int32, planes.shape, 0)
    return jnp.sum(jnp.where(which == at, planes, 0.0), axis=0)


def pair_rows(scr, first, stride, count):
    even = scr[pl.ds(first, count, stride=2 * stride), :]
    odd = scr[pl.ds(first + stride, count, stride=2 * stride), :]
    return jnp.concatenate([even, odd], axis=1)


def selector(lift, count, first, features_in):
    shape = (MODES * features_in, count * CH)
    rows = lax.broadcasted_iota(jnp.int32, shape, 0)
    cols = lax.broadcasted_iota(jnp.int32, shape, 1)
    tiled = jnp.concatenate([lift] * MODES, axis=0) if features_in > 1 else lift
    tiled = jnp.concatenate([tiled] * count, axis=1)
    mode = sum((cols >= CH * m).astype(jnp.int32) for m in range(1, count))
    kz = lax.shift_right_logical(rows, 2) if features_in > 1 else rows
    return jnp.where(kz == first + mode, tiled, 0.0)


K0 = math.sqrt(2.0 / math.pi)


def gelu_parts(x):
    x2 = x * x
    half = 0.5 + 0.5 * jnp.tanh(x * (K0 + (0.044715 * K0) * x2))
    slope = half + x * (2.0 * K0 + (6.0 * 0.044715 * K0) * x2) * (half - half * half)
    return x * half, slope


def block_pre(bb, b, zi):
    rows = bb.shape[0] // 2
    lanes = slice(MODES * CL * b, MODES * CL * (b + 1))
    return mm(bb[:rows, lanes], zi[: MODES * CL]) + mm(bb[rows:, lanes], zi[MODES * CL :])


def lanes_of(row, b, tile):
    return mmh(row[:, CL * b : CL * (b + 1)], tile)


def point_block(point, b, tile, shift):
    count = point.shape[0]
    full = jnp.concatenate([lanes_of(point, b, tile)] * ZP, axis=0)
    z_row = lax.shift_right_logical(lax.broadcasted_iota(jnp.int32, full.shape, 0), shift)
    z_col = lax.shift_right_logical(lax.broadcasted_iota(jnp.int32, full.shape, 1), 3)
    return jnp.where(z_row == z_col, full, 0.0).astype(BF)


def split(x):
    top = x.astype(BF)
    return top, (x - top.astype(F32)).astype(BF)


def mm_split(x, table):
    top, low = split(x)
    return mm(top, table) + mm(low, table)


def mm_split_right(table, x):
    top, low = split(x)
    return mm(table, top) + mm(table, low)


def put_block(a_scr, gp, b, zf):
    a = mm(gp, zf).astype(BF)
    rows = a.shape[0]
    width = MODES * CL
    a_scr[:rows, width * b : width * (b + 1)] = a[:, :width]
    a_scr[rows:, width * b : width * (b + 1)] = a[:, width:]


def forward_tail(a_scr, table, perm):
    return mm(mm(table, a_scr[...]).astype(BF), perm)


def here():
    return lax.axis_index("level"), lax.axis_index("wide")


def greet():
    level, wide = here()
    barrier = pltpu.get_barrier_semaphore()
    for i in range(1, LV):
        pl.semaphore_signal(barrier, inc=1, device_id=(lax.rem(level + i, LV), wide), device_id_type=MESH)

    def one(i, carry):
        pl.semaphore_signal(barrier, inc=1, device_id=(level, lax.rem(wide + i, WD)), device_id_type=MESH)
        return carry

    lax.fori_loop(1, WD, one, 0)
    return barrier, LV - 1 + WD - 1


def remote(src, dst, sems, to):
    return pltpu.make_async_remote_copy(
        src_ref=src, dst_ref=dst, send_sem=sems.at[0], recv_sem=sems.at[1], device_id=to, device_id_type=MESH)


def push_wide(source, land, sems):
    level, wide = here()

    def one(i, carry):
        peer = lax.rem(wide + i, WD)
        remote(source(peer), land.at[wide], sems, (level, peer)).start()
        return carry

    lax.fori_loop(1, WD, one, 0)


def push_level(source, land, sems):
    level, wide = here()
    for i in range(1, LV):
        peer = lax.rem(level + i, LV)
        remote(source(peer), land.at[level], sems, (peer, wide)).start()


def push_y(source, land, sems):
    level, wide = here()
    for i in range(1, 4):
        peer = lax.rem(wide + 16 * i, WD)
        remote(source, land.at[wide // 16], sems, (level, peer)).start()


def push_zc(source, land, sems):
    level, wide = here()
    base = 16 * (wide // 16)

    def one(i, carry):
        peer = lax.rem(wide + i, 16)
        remote(source(peer), land.at[wide % 16], sems, (level, base + peer)).start()
        return carry

    lax.fori_loop(1, 16, one, 0)


def finish(land, sems, count):
    level, wide = here()
    part = land.at[pl.ds(0, count - 1)]
    done = remote(part, part, sems, (level, wide))
    done.wait_send()
    done.wait_recv()


SEMS = dict(
    in_level=2, inw=2, g=2, g_level=2, rows=2, spec=2, box1=2, box2=2, f=2, dual=2, pt1=2, pt2=2, q=2, q_level=2,
    pt_level=2, out_level=2, got_g=2, out=2,
)
RESULTS = dict(
    grad_f=((8, KF, 2, CC), F32), s_g=((4 * KF, 2 * CH), F32), got_g=((WD, 8, 128), BF),
    coarse=((PG, YG * GZ), BF), fine=((1, PF, FY * FZ), BF),
)
LANDS = dict(
    in_level=((LV, 8, PG, 128), F32), inw=((WD, 8, 128), BF),
    g=((LV, WD, 8, 128), BF), rows=((LV, 128, 128), BF), spec=((WD, 1, 128), F32),
    box1=((4, PG, 32, 128), BF), box2=((16, 32, 128), BF), f=((WD, 16, 128), BF), dual=((WD, 16, 128), BF), pt1=((16, 32, 128), BF), pt2=((4, PG, 32, 128), BF),
    q=((LV, WD, 1, 128), F32), pt_level=((LV, 128, 128), BF), out_level=((LV, 64, MODES * CH), BF),
)
LANDED = "_land"
SCRATCH = dict(
    x_g=((256, GZ * 4), F32), x_ff=((256, FZ * 4), F32), feat_g=((256, GZ * 4), BF), feat_f=((256, FZ * 4), BF),
    kg=((KF, PG, 128), F32), kf=((KF, PF, 128), F32), cot_f=((256, FZ), F32),
    msg_in=((WD, 8, 128), F32), msg_b=((WD, 8, 128), BF), p_gm=((WD, 8, 128), BF), mix_a=((512, CHUNK), F32), mix_b=((512, CHUNK), F32),
    mix_ga=((128, CHUNK), F32), mix_gb=((128, CHUNK), F32), wide_cot=((256, ZP * CL), F32),
    x_wide=((KF, 8, 8, 128), F32), x_in=((256, 1024), BF), acc=((256, ZP * CL), F32),
    acc_pt=((256, ZP * CL), F32), slope=((NB, 256, ZP * CL), BF), pred_b=((128, 128), BF), pred_g=((256, ZP), F32), pred_f=((256, FZ), F32),
    box_f=((256, ZP), F32), s_box=((2 * KF * PG, MODES), F32),
    o_box=((KF, 128), F32), spec_m=((KF, 1, 128), F32), planes_m=((PG, 32, 128), BF),
    x_box=((GX, 2 * MODES), F32), p_f=((4 * 2 * FX, 128), F32), p_fm=((WD, 16, 128), BF),
    v_f=((8 * 2 * KF, CH), F32), pre_g=((NB, 256, ZP * CL), F32), pre_f=((NB, 256, ZP * CL), F32),
    pre_p=((2 * FX, 512), F32), v_lanes=((2 * KF, 512), F32), s_f=((4 * KF, 8 * CH), F32), dual_f=((4 * KF, 512), F32), x_f=((KF, 32, 128), F32), x_fb=((128, 1024), BF),
    a=((512, MODES * CH), BF), m_f=((KF, 32, 128), F32), m_fm=((WD, 16, 128), BF),
    pt=((FY // 2, ZP), F32), pt_m=((32, 128), BF), d_f=((4 * 2 * FX, 128), F32),
    d_lanes=((2 * FX, 512), BF), q_rows=((2 * GX, 8), F32),
    q_m=((WD, 1, 128), F32), mine=((128, 128), BF), box_m=((16, 32, 128), BF), pt_mid=((PG, 32, 128), BF), gf=((8, KF, 2, CC), F32), cot=((256, ZP), F32),
    send_g=((LV, 64, MODES * CH), BF), msg_out=((8, 8, 8, 128), F32), msg_ob=((8, 8, 8, 128), BF), out_g=((PG, YG * GZ), F32), out_f=((PF, FY * FZ), F32),
)

def chain_body(scalars, start, get, res, scr, sem):
    level, wide = here()
    start(6)
    land = Names(**{n: getattr(scr, n + LANDED) for n in LANDS})
    corner = scalars.well_x[level]
    rows_at = scalars.well_y[level]
    barrier, count = greet()
    kg, kf = scr.kg, scr.kf
    features(FY, PF, FZ * 4, get.x_in_f, get.z4_f[...], get.tya_f[...], scr.feat_f, kf, scr.x_ff)
    features(YG, PG, GZ * 4, get.x_in_g, get.z4_g[...], get.tya_g[...], scr.feat_g, kg, scr.x_g)
    pl.semaphore_wait(barrier, count)

    push_level(lambda peer: kg.at[pl.ds(8 * peer, 8)], land.in_level, sem.in_level)
    start(None)
    land.in_level[level] = kg[pl.ds(8 * level, 8)]
    msg = scr.msg_in
    msg[...] = jnp.zeros(msg.shape, F32)
    for w in range(WD):
        msg[w, PG : PG + PF, :] = kf[w // 2]
    finish(land.in_level, sem.in_level, LV)
    total = land.in_level[0] + land.in_level[1] + land.in_level[2] + land.in_level[3]
    for w in range(WD):
        msg[w, :PG, :] = total[w // 8]
    msg_b = scr.msg_b
    msg_b[...] = msg[...].astype(BF)
    push_wide(lambda peer: msg_b.at[peer], land.inw, sem.inw)
    land.inw[wide] = msg_b[wide]
    tile = get.tile[...]
    lift_g, lift_f = get.lift_g[...].astype(F32), get.lift_f[...].astype(F32)
    point_g = mmh(lift_g, get.mix_g[...].astype(F32))
    point_f = mmh(lift_f, get.mix_f[...].astype(F32))
    ro_g, ro_f = get.ro_g[...].astype(F32), get.ro_f[...].astype(F32)
    spread, fold = get.spread, get.fold[...]
    lift_lanes = mm(get.lift_f[...], spread[...])[4:5, :]
    ro_gl = [lanes_of(ro_g, b, tile) for b in range(NB)]
    ro_fl = [lanes_of(ro_f, b, tile) for b in range(NB)]
    v_fl = [lanes_of(point_f[4:5], b, tile) for b in range(NB)]
    for b in range(NB):
        scr.pre_g[b] = mm(scr.feat_g[...], point_block(point_g, b, tile, 2)[: GZ * 4])
    w_f, w_g = get.w_f, get.w_g
    acc = scr.mix_a
    for c in range(CC // CHUNK):
        part = weights_chunk(w_f, c) * lift_lanes[:, CHUNK * c : CHUNK * (c + 1)]
        if c == 0:
            acc[...] = part
        else:
            acc[...] += part
    scr.v_f[...] = mm_split(acc[...], fold)
    scr.v_lanes[...] = jnp.zeros(scr.v_lanes.shape, F32)
    for m in range(8):
        scr.v_lanes[:, lane_f(m) : lane_f(m) + CH] = scr.v_f[2 * KF * m : 2 * KF * (m + 1), :]
    finish(land.inw, sem.inw, WD)

    u = halves(land.inw[...].astype(F32).reshape(WD * 8, 128))
    s = mmh(mmh(get.txs_g[...], u), selector(lift_g, 2, 2 * lax.rem(wide, 8), 4))
    p_gm = scr.p_gm
    p_gm_rows = mix_modes(s, 2, w_g, spread, fold, get.txb_g[...], scr.mix_ga, scr.mix_gb)
    p_gm[...] = p_gm_rows.reshape(p_gm.shape).astype(BF)
    own_g = land.g.at[level]
    push_wide(lambda peer: p_gm.at[peer], own_g, sem.g)
    own_g[wide] = p_gm[wide]
    res.s_g[...] = s
    first = 8 * lax.rem(wide, 2)
    s_f = mmh(mmh(get.txs_f[...], u), selector(lift_f[:4], 8, first, 4))
    finish(own_g, sem.g, WD)
    push_level(lambda peer: own_g, land.g, sem.g_level)
    scr.pre_p[...] = mix_modes(s_f, 8, w_f, spread, fold, get.txb_f[...], scr.mix_a, scr.mix_b)
    sel_c = selector(lift_f[4:5], 8, first, 1)
    sel_u = lax.broadcasted_iota(jnp.int32, (MODES, 512), 0) == first + lanes_of_modes((MODES, 512))
    sel_u = jnp.where(sel_u, 1.0, 0.0)
    for b in range(NB):
        scr.pre_f[b] = mm(scr.feat_f[...], point_block(point_f[:4], b, tile, 2))
    cot_in = get.cot_in_f
    for y in range(FY):
        scr.cot_f[PF * y : PF * (y + 1), :] = cot_in[:, FZ * y : FZ * (y + 1)]
    ones_cl = get.ones_cl[...]
    scr.wide_cot[...] = mm_split(scr.cot_f[...], ones_cl)
    cot, cot_in = scr.cot, get.cot_in_g
    cot[...] = jnp.zeros(cot.shape, F32)
    for y in range(YG):
        cot[PG * y : PG * (y + 1), :GZ] = cot_in[:, GZ * y : GZ * (y + 1)]
    finish(land.g, sem.g_level, LV)

    scr.x_wide[...] = land.g[...].astype(F32).reshape(KF, 8, 8, 128)
    for q in range(8):
        scr.x_in[:, 128 * q : 128 * (q + 1)] = scr.x_wide[:, q].reshape(256, 128).astype(BF)
    perm_in = get.perm_in[...]
    bb = mm(get.tyi_g[...], mm(scr.x_in[...], perm_in).astype(BF)).astype(BF)
    zi = get.zi_g[...]
    acc, acc_pt = scr.acc, scr.acc_pt
    for b in range(NB):
        pre = block_pre(bb, b, zi) + scr.pre_g[b]
        hidden, slope = gelu_parts(pre)
        scr.slope[b] = slope.astype(BF)
        part = hidden * ro_gl[b]
        if b == 0:
            acc[...] = part
        else:
            acc[...] += part
    sum_cl = get.sum_cl[...]
    pred = mm_split(acc[...], sum_cl)
    scr.pred_b[...] = jnp.concatenate([pred[:128], pred[128:]], axis=1).astype(BF)
    push_level(lambda peer: scr.pred_b, land.rows, sem.rows)
    land.rows[level] = scr.pred_b[...]
    scr.pred_g[...] = pred
    pick_box = [pick_packed(8 * PG * rows_at, h) for h in range(2)]
    finish(land.rows, sem.rows, LV)

    rows = land.rows[...].reshape(LV * 128, 128)
    box = mm(pick_box[0], rows[:, :ZP]) + mm(pick_box[1], rows[:, ZP:])
    a = mmh(box, get.zc[...])
    scr.s_box[...] = mmh(get.tya_box[...], halves(a))
    for p in range(PG):
        for r in range(2):
            at = 2 * MODES * p + MODES * r
            scr.o_box[:, at : at + MODES] = scr.s_box[pl.ds(KF * PG * r + p, KF, stride=PG), :]
    spec_m, planes_m = scr.spec_m, scr.planes_m
    spec_m[...] = scr.o_box[...].reshape(spec_m.shape)
    push_wide(lambda peer: spec_m.at[peer // 2], land.spec, sem.spec)
    land.spec[wide] = spec_m[wide // 2]
    scr.box_f[...] = box
    for p in range(PG):
        planes_m[p] = pair_rows(scr.box_f, p, PG, FY // 4).astype(BF)
    push_y(planes_m, land.box1, sem.box1)
    y_me, zc_me = wide // 16, wide % 16
    land.box1[y_me] = planes_m[...]
    pick_x = shift_rows(FX // 2, GX, corner)
    txs_box = get.txs_box[...]
    txs_box = jnp.concatenate([mmh(txs_box[:, : FX // 2], pick_x), mmh(txs_box[:, FX // 2 :], pick_x)], axis=1)
    vv = jnp.concatenate([scr.v_lanes[...]] * 2, axis=0)
    finish(land.box1, sem.box1, 4)
    which = lax.broadcasted_iota(jnp.int32, (16, 32, 128), 0) + 16 * y_me
    box_m = jnp.zeros((16, 32, 128), F32)
    for p in range(PG):
        plane = jnp.zeros((32, 128), F32)
        for y in range(4):
            at = 64 * y + 4 * zc_me + p - corner
            inside = jnp.logical_and(at >= 0, at < WD).astype(jnp.int32)
            plane += where_at(jnp.zeros((32, 128), jnp.int32) + inside, 1, land.box1[y, p].astype(F32))
        box_m += where_at(which, lax.rem(4 * zc_me + p - corner + 4 * WD, WD), plane[None])
    scr.box_m[...] = box_m.astype(BF)
    push_zc(lambda peer: scr.box_m.at[peer], land.box2, sem.box2)
    land.box2[zc_me] = scr.box_m[zc_me]
    finish(land.spec, sem.spec, WD)

    got = land.spec[...].reshape(WD, 128)
    for p in range(PG):
        scr.x_box[pl.ds(p, WD, stride=PG), :] = got[:, 2 * MODES * p : 2 * MODES * (p + 1)]
    uc = mmh(txs_box, halves(scr.x_box[...]))
    value = scr.pre_p[...] + mm_split_right(get.txb_f[...], mmh(uc, sel_u) * vv)
    p_f, p_fm = scr.p_f, scr.p_fm
    for k in range(4):
        p_f[pl.ds(k, 2 * FX, stride=4), :] = value[:, 128 * k : 128 * (k + 1)]
    p_fm[...] = p_f[...].astype(BF).reshape(p_fm.shape)
    push_wide(lambda peer: p_fm.at[peer], land.f, sem.f)
    land.f[wide] = p_fm[wide]
    scr.s_f[...] = s_f + mmh(uc, sel_c)
    lc_f = [point_block(point_f[4:5], b, tile, 0) for b in range(NB)]
    finish(land.box2, sem.box2, 16)
    plane = jnp.sum(land.box2[...].astype(F32), axis=0).astype(BF)
    rows_up = get.rows_up
    rows = mm(rows_up[0], plane[:, :ZP]) + mm(rows_up[1], plane[:, ZP:])
    cl = mm(rows.astype(BF), get.z_up[...]).astype(BF)
    for b in range(NB):
        scr.pre_f[b] += mm(cl, lc_f[b])
    finish(land.f, sem.f, WD)

    scr.x_f[...] = land.f[...].astype(F32).reshape(KF, 32, 128)
    for g in range(8):
        lanes = scr.x_f[:, pl.ds(16 * (g // 4) + g % 4, 4, stride=4), :]
        scr.x_fb[:, 128 * g : 128 * (g + 1)] = lanes.reshape(128, 128).astype(BF)
    bb = mm(get.tyi_f[...], mm(scr.x_fb[...], perm_in).astype(BF)).astype(BF)
    zi, zf = get.zi_f[...], get.zf_f[...]
    for b in range(NB):
        pre = block_pre(bb, b, zi) + scr.pre_f[b]
        hidden, slope = gelu_parts(pre)
        ro_lanes = ro_fl[b]
        gp = (slope * (scr.wide_cot[...] * ro_lanes)).astype(BF)
        part = hidden * ro_lanes
        part_pt = gp.astype(F32) * v_fl[b]
        if b == 0:
            acc[...] = part
            acc_pt[...] = part_pt
        else:
            acc[...] += part
            acc_pt[...] += part_pt
        put_block(scr.a, gp, b, zf)
    z = forward_tail(scr.a, get.tyf_f[...], get.perm_wide[...])
    m_f, m_fm = scr.m_f, scr.m_fm
    for g in range(8):
        m_f[:, pl.ds(16 * (g // 4) + g % 4, 4, stride=4), :] = z[:, 128 * g : 128 * (g + 1)].reshape(KF, 4, 128)
    m_fm[...] = m_f[...].astype(BF).reshape(m_fm.shape)
    push_wide(lambda peer: m_fm.at[peer], land.dual, sem.dual)
    land.dual[wide] = m_fm[wide]
    point = mm_split(acc_pt[...], sum_cl)
    scr.pt[...] = mmh(mmh(get.rows_down[...], point), get.z_down[...])
    pt_m = scr.pt_m
    pt_m[...] = pair_rows(scr.pt, 0, 1, FY // 4).astype(BF)
    push_zc(lambda peer: pt_m, land.pt1, sem.pt1)
    land.pt1[zc_me] = pt_m[...]
    scr.pred_f[...] = mm_split(acc[...], sum_cl)
    place_x = mmh(shift_rows(2 * GX, FX, -2 * corner), get.txb_box[...])
    which = lax.broadcasted_iota(jnp.int32, (16, 32, 128), 0)
    finish(land.pt1, sem.pt1, 16)
    planes = land.pt1[...].astype(F32)
    for p in range(PG):
        at = lax.rem(4 * zc_me + p - corner - 16 * y_me + 8 * WD, WD)
        scr.pt_mid[p] = jnp.sum(where_at(which, at, planes), axis=0).astype(BF)
    push_y(scr.pt_mid, land.pt2, sem.pt2)
    land.pt2[y_me] = scr.pt_mid[...]
    finish(land.dual, sem.dual, WD)

    d_f, d_lanes = scr.d_f, scr.d_lanes
    d_f[...] = land.dual[...].astype(F32).reshape(d_f.shape)
    for g in range(4):
        d_lanes[:, 128 * g : 128 * (g + 1)] = d_f[pl.ds(g, 2 * FX, stride=4), :].astype(BF)
    z = mm(get.txd_f[...], d_lanes[...])
    rows = 2 * KF
    zc, zd = z[2 * rows : 3 * rows], z[3 * rows :]
    cols = []
    for m in range(8):
        v = scr.v_f[rows * m : rows * (m + 1), :]
        lanes = slice(lane_f(m), lane_f(m) + CH)
        cols.append(jnp.concatenate([
            jnp.sum(v * zc[:, lanes], axis=1, keepdims=True),
            jnp.sum(v * zd[:, lanes], axis=1, keepdims=True)], axis=0))
    q_rows, q_m = scr.q_rows, scr.q_m
    q_rows[...] = mmh(place_x, jnp.concatenate(cols, axis=1))
    lanes = [q_rows[pl.ds(r, WD, stride=8), :] for r in range(8)]
    lanes.append(jnp.zeros((WD, 64), F32))
    q_m[...] = jnp.concatenate(lanes, axis=1).reshape(q_m.shape)
    own = land.q.at[level]
    push_wide(lambda peer: q_m.at[peer], own, sem.q)
    own[wide] = q_m[wide]
    scr.dual_f[...] = z[: 2 * rows]
    finish(land.pt2, sem.pt2, 4)
    mine = scr.mine
    which = lax.broadcasted_iota(jnp.int32, (4, 32, 128), 0)
    for p in range(PG):
        at = PG * wide + p - corner
        at = jnp.where(jnp.logical_and(at >= 0, at < WD), lax.shift_right_logical(at, 4), 4)
        planes = where_at(which, at, land.pt2[:, p].astype(F32))
        mine[32 * p : 32 * (p + 1), :] = jnp.sum(planes, axis=0).astype(BF)
    push_level(lambda peer: mine, land.pt_level, sem.pt_level)
    land.pt_level[level] = mine[...]
    finish(own, sem.q, WD)
    push_level(lambda peer: own, land.q, sem.q_level)
    tyb = get.tyb_box[...]
    tables = []
    for l in range(LV):
        tables.append(mm(shift_rows(YG, FY // 2, YG * level - 8 * scalars.well_y[l]).astype(BF), tyb).astype(BF))
    finish(land.pt_level, sem.pt_level, LV)
    planes = jnp.zeros((128, 128), F32)
    for l in range(LV):
        move = shift_rows(128, 128, 32 * level - 4 * scalars.well_y[l], 32).astype(BF)
        planes += mm(move, land.pt_level[l])
    for p in range(PG):
        for k in range(2):
            part = planes[32 * p : 32 * (p + 1), ZP * k : ZP * (k + 1)]
            cot[pl.ds(PG * k + p, 32, stride=2 * PG), :] += part
    finish(land.q, sem.q_level, LV)

    q = land.q[...].reshape(LV * WD, 128)[:, :64]
    odd = jnp.bitwise_and(lax.broadcasted_iota(jnp.int32, q.shape, 0), 1) == 1
    q = jnp.concatenate([jnp.where(odd, 0.0, q), jnp.where(odd, q, 0.0)], axis=1).astype(BF)
    g = mm(q, get.dd_box[...]).astype(BF)
    total = jnp.zeros((YG, PG * ZP), F32)
    for l in range(LV):
        part = g[WD * l : WD * (l + 1)]
        part = jnp.concatenate([part[:, PG * ZP * k : PG * ZP * (k + 1)] for k in range(4)], axis=0)
        total += mm(tables[l], part)
    for p in range(PG):
        cot[pl.ds(p, YG, stride=PG), :] += total[:, ZP * p : ZP * (p + 1)]
    wide_cot = mm_split(cot[...], ones_cl)
    zf = get.zf_g[...]
    for b in range(NB):
        gp = (scr.slope[b].astype(F32) * (wide_cot * ro_gl[b])).astype(BF)
        put_block(scr.a, gp, b, zf)
    send_g = scr.send_g
    send_g[...] = forward_tail(scr.a, get.tyf_g[...], get.perm_out[...]).astype(BF).reshape(send_g.shape)
    push_level(lambda peer: send_g.at[peer], land.out_level, sem.out_level)
    land.out_level[level] = send_g[level]
    msg = scr.msg_out
    msg[...] = jnp.zeros(msg.shape, F32)
    for y in range(YG):
        scr.out_g[:, GZ * y : GZ * (y + 1)] = scr.pred_g[PG * y : PG * (y + 1), :GZ]
    res.coarse[...] = scr.out_g[...].astype(BF)
    for y in range(FY):
        scr.out_f[:, FZ * y : FZ * (y + 1)] = scr.pred_f[PF * y : PF * (y + 1), :]
    res.fine[0] = scr.out_f[...].astype(BF)
    finish(land.out_level, sem.out_level, LV)
    out = land.out_level
    total = out[0].astype(F32) + out[1].astype(F32) + out[2].astype(F32) + out[3].astype(F32)
    for q in range(8):
        msg[:, q, :, : 2 * CH] = total[:, 2 * CH * q : 2 * CH * (q + 1)].reshape(8, 8, 2 * CH)
    msg_ob = scr.msg_ob
    msg_ob[...] = msg[...].astype(BF)
    push_wide(lambda peer: msg_ob.at[peer // 8, peer % 8], res.got_g, sem.got_g)
    res.got_g[wide] = msg_ob[wide // 8, wide % 8]
    copies = []
    tile_out = get.tile_out[...]
    for k in range(2):
        buf = scr.gf.at[pl.ds(4 * k, 4)]
        d = scr.dual_f[:, 256 * k : 256 * (k + 1)]
        part = scr.s_f[:, 4 * CH * k : 4 * CH * (k + 1)]
        grads(part, stack_modes(d[: 2 * KF], 4, lane_f), stack_modes(d[2 * KF :], 4, lane_f), 4, spread, tile_out, buf)
        copies.append(pltpu.make_async_copy(buf, res.grad_f.at[pl.ds(4 * k, 4)], sem.out.at[k]))
        copies[-1].start()
    finish(res.got_g, sem.got_g, WD)
    for copy in copies:
        copy.wait()


def last_body(scalars, start, get, res, scr, sem):
    ins, outs = [], []
    for k in range(4):
        part = pl.ds(2 * k, 2)
        ins.append(pltpu.make_async_copy(get.grad_f.at[part], scr.buf.at[part], scr.sem_in.at[k]))
        outs.append(pltpu.make_async_copy(scr.buf.at[part], res.grad_f.at[part], scr.sem_out.at[k]))
        ins[k].start()
    start(None)
    for k in range(4):
        ins[k].wait()
        outs[k].start()
    rows = 2 * KF
    z = mm(get.txd_g[...], get.got_g[...].astype(F32).reshape(2 * GX, 128).astype(BF))
    za, zb = stack_modes(z[:rows], 2, lane_f), stack_modes(z[rows:], 2, lane_f)
    grads(get.s_g[...], za, zb, 2, get.spread, get.tile_out[...], res.grad_g)
    res.coarse[...] = get.coarse[...]
    res.fine[...] = get.fine[...]
    for copy in outs:
        copy.wait()


CHAIN_TABLES = dict(
    z4_f=Z4_F, tya_f=TYA_F, z4_g=Z4_G, tya_g=TYA_G,
    tile=TILE_CL, spread=SPREAD_IN, fold=FOLD, txs_g=TXS_G, txb_g=TXB_G, txs_f=TXS_F,
    ones_cl=ONES_CL, perm_in=PERM_WIDE, tyi_g=TYI_G, zi_g=ZI_G, sum_cl=SUM_CL, zc=ZC,
    tya_box=TYA_BOX, txs_box=TXS_BOX, txb_f=TXB_F, rows_up=ROWS_UP, z_up=Z_UP, tyi_f=TYI_F,
    zi_f=ZI_F, zf_f=ZF_F, tyf_f=TYF_F, perm_wide=PERM_WIDE_OUT, rows_down=ROWS_DOWN, z_down=Z_DOWN,
    txd_f=TXD_F, txb_box=TXB_BOX, tyb_box=TYB_BOX, dd_box=DD_BOX, zf_g=ZF_G, tyf_g=TYF_G,
    perm_out=PERM_OUT, tile_out=TILE_OUT,
)

def shards(coarse_input, fine_input, coarse_cotangent, fine_cotangent, well_x, well_y, coarse_lift, coarse_mixing,
           coarse_spectral, coarse_readout, fine_lift, fine_mixing, fine_spectral, fine_readout):
    tables = {n: jnp.asarray(t) for n, t in CHAIN_TABLES.items()}
    first = [n for n in tables][:4]
    inputs = dict(
        x_in_f=fine_input[0], x_in_g=coarse_input, **{n: tables.pop(n) for n in first},
        lift_g=coarse_lift, lift_f=fine_lift[0], mix_g=coarse_mixing, mix_f=fine_mixing[0], ro_g=coarse_readout[None],
        ro_f=fine_readout, w_f=fine_spectral[0], w_g=coarse_spectral, cot_in_f=fine_cotangent[0],
        cot_in_g=coarse_cotangent, **tables)
    scratch = {**{n + LANDED: v for n, v in LANDS.items()}, **SCRATCH}
    res = run(chain_body, RESULTS, dict(well_x=well_x, well_y=well_y), inputs, scratch, SEMS, kept=1, cid=1, name="chain")
    inputs = dict(
        grad_f=res.grad_f, got_g=res.got_g, s_g=res.s_g, spread=jnp.asarray(SPREAD_IN), tile_out=jnp.asarray(TILE_OUT),
        txd_g=jnp.asarray(TXD_G), coarse=res.coarse, fine=res.fine)
    out = run(
        last_body,
        dict(grad_f=((8, KF, 2, CC), F32), grad_g=((2, KF, 2, CC), F32), coarse=((PG, YG * GZ), BF),
             fine=((1, PF, FY * FZ), BF)),
        {}, inputs, dict(buf=((8, KF, 2, CC), F32), sem_in=4, sem_out=4), kept=1, passed=list(inputs)[:1], name="last")
    return out.coarse, out.fine, out.grad_g, out.grad_f[None]


def solution(mesh):
    placed = (
        P("wide", "level"),
        P("level", "wide", None),
        P("wide", "level"),
        P("level", "wide", None),
        P(),
        P(),
        P(),
        P(),
        P(("level", "wide"), None, None, None),
        P(),
        P("level", None, None),
        P("level", None, None),
        P("level", "wide", None, None, None),
        P("level", None),
    )
    return jax.shard_map(
        shards,
        mesh=mesh,
        in_specs=placed,
        out_specs=(
            P("wide", "level"),
            P("level", "wide", None),
            P(("level", "wide"), None, None, None),
            P("level", "wide", None, None, None),
        ),
        check_vma=False,
    )
```

time: 139 us -> 119 us (0.86)
  Pallas kernels: 138 us -> 118 us
    pallas_call x2, Pallas kernels: 138 us -> 118 us  [run(): pl.pallas_call(kernel, out_shape=[jax.ShapeDtypeStruct(s, d) for s, d in...]
where the time goes in v3:
time: 119 us
  Pallas kernels  118 us (99%)
    pallas_call x2, Pallas kernels, run(): pl.pallas_call(kernel, out_shape=[jax.ShapeDtypeStruct(s, d) for s, d in...  118 us

profile of v3, /device:TPU:1, one launch (start us, length us, event | category | flops | bytes accessed | tf_op | source)
XLA Modules:
  0.0 119.2 jit_solution(17888071260569545872)
XLA Ops:
  0.6 113.0 %chain.1 = (f32[8,32,2,2304]{3,2,1,0:T(2,128)}, f32[128,96]{1,0:T(8,128)}, bf16[64,8,128]{2,1,0:T(8,128)(2,1)}, bf16[4,3200]{1,0:T(4,128)(2,1)}, bf16[1,2,8192]{2,1,0:T(2,128)(2,1)}) custom-call(s32[4]{0:T(128)} %refs_0_.1, s32[4]{0:T(128)} %refs_1_.1, bf16[2,32768]{1,0:T(2,128)(2,1)} %bitcast.8, bf16[4,12800]{1,0:T(4,128)(2,1)} %refs_3_.2, ...), custom_call_target="tpu_custom_call" | custom-call | tf_op jit(solution)/shard_map/chain/pallas_call | solution.py:226
  113.6 5.4 %last.1 = (f32[8,32,2,2304]{3,2,1,0:T(2,128)}, f32[2,32,2,2304]{3,2,1,0:T(2,128)}, bf16[4,3200]{1,0:T(4,128)(2,1)}, bf16[1,2,8192]{2,1,0:T(2,128)(2,1)}) custom-call(f32[8,32,2,2304]{3,2,1,0:T(2,128)} %get-tuple-element.13.refs_0_, bf16[64,8,128]{2,1,0:T(8,128)(2,1)} %get-tuple-element.14.refs_1_, f32[128,96]{1,0:T(8,128)} %get-tuple-element.15.refs_2_, ...), custom_call_target="tpu_custom_call" | custom-call | tf_op jit(solution)/shard_map/last/pallas_call | solution.py:226
